TPU v7x, 512 devices: a whole 4x8x8 slice. The times are simulated.
512 devices in a mesh: dp: 32 (over y, x), mp: 16 (over z, core).
Axes of the slice: x: 4, y: 8, z: 8, core: 2. Of those that a mesh axis runs over, the one named last changes fastest.
Arguments:
- activations: bfloat16 [24, 512, 32768], P(None, 'mp', 'dp'), may hold values from -6 to 6
- cotangent: bfloat16 [32768, 1024], P('dp'), may hold values from -0.0078125 to 0.0078125
- slot_blocks: int32 [64], replicated, may hold values from 0 to 48, as said below
- left_stat: float32 [64, 512, 512], P('dp', 'mp'), may hold values from -6 to 48
- right_stat: float32 [64, 512, 512], P('dp', 'mp'), may hold values from -6 to 48
- left_root: bfloat16 [64, 512, 512], P('dp', 'mp'), may hold values from -1 to 1.5
- right_root: bfloat16 [64, 512, 512], P('dp', 'mp'), may hold values from -1 to 1.5
Outputs:
- left_new: float32 [64, 512, 512], P('dp', 'mp')
- right_new: float32 [64, 512, 512], P('dp', 'mp')
- precond: bfloat16 [64, 512, 512], P('dp')
Inputs may be any that keep to these rules, and one draw needn't show every extreme that they name: `slot_blocks`: slots k * 2 to k * 2 + 1 belong to owner k. Every block number below 48 stands in exactly one slot; the value 48 marks an empty slot; owners hold different numbers of blocks, and some owner has all 2 slots filled.
All inputs are finite; a program needn't handle non-finite values.
Results may differ from a plain program's by a relative error of at most 0.024.
Values may be sent and summed in bfloat16 or wider, within the bound.
No kernel may reach another device: no remote copies, remote signals or barrier semaphores. Data moves between devices by JAX's collectives and lax.ppermute only.
A program may use at most 192 MiB of HBM per device.

v0:
```python
import jax
import jax.numpy as jnp
from jax import lax
from jax.sharding import PartitionSpec as P

COL_BLOCKS = 2


decay_factor = 0.95


def local(activations, cotangent, slot_blocks, left_stat, right_stat, left_root, right_root):
    row_blocks, shard_rows, tok_count = activations.shape
    block_width = cotangent.shape[1] // COL_BLOCKS
    block_total = row_blocks * COL_BLOCKS
    slot_count = left_stat.shape[0]
    cot_blocks = cotangent.reshape(tok_count, COL_BLOCKS, block_width)
    owner_index = lax.axis_index("dp")
    own_ids = lax.dynamic_slice_in_dim(slot_blocks, owner_index * slot_count, slot_count)
    partial_grad = jnp.einsum(
        "irt,tjc->ijrc", activations, cot_blocks, preferred_element_type=jnp.float32
    )
    partial_grad = partial_grad.reshape(block_total, shard_rows, block_width)
    summed = lax.psum(partial_grad.astype(jnp.bfloat16), "dp").astype(jnp.float32)
    is_live = own_ids < block_total
    picked = jnp.take(summed, jnp.minimum(own_ids, block_total - 1), axis=0)
    grad = jnp.where(is_live[:, None, None], picked, 0.0)
    grad_b = grad.astype(jnp.bfloat16)
    col_start = lax.axis_index("mp") * shard_rows
    shard_piece = lax.all_gather(grad_b, "mp", axis=1, tiled=True)
    left_part = jnp.einsum("srb,spb->srp", grad_b, shard_piece, preferred_element_type=jnp.float32)
    left_cols = left_part
    own_cols = lax.dynamic_slice_in_dim(shard_piece, col_start, shard_rows, 2)
    right_rows = jnp.einsum(
        "spr,spb->srb", own_cols, shard_piece, preferred_element_type=jnp.float32
    )
    root_part = left_root
    lifted = jnp.einsum("srp,spb->srb", root_part, shard_piece, preferred_element_type=jnp.float32)
    left_cols, right_rows, lifted = (left_cols, right_rows, lifted)
    left_new = decay_factor * left_stat + left_cols
    right_new = decay_factor * right_stat + right_rows
    lifted_b = lifted.astype(jnp.bfloat16)
    root_part = lifted_b
    right_applied = jnp.einsum(
        "srp,spb->srb",
        root_part,
        lax.all_gather(right_root, "mp", axis=1, tiled=True),
        preferred_element_type=jnp.float32,
    )
    precond = lax.all_gather(right_applied.astype(jnp.bfloat16), "mp", axis=1, tiled=True)
    return (left_new, right_new, precond)


def solution(mesh):
    return jax.shard_map(
        local,
        mesh=mesh,
        in_specs=(
            P(None, "mp", "dp"),
            P("dp", None),
            P(),
            P("dp", "mp", None),
            P("dp", "mp", None),
            P("dp", "mp", None),
            P("dp", "mp", None),
        ),
        out_specs=(P("dp", "mp", None), P("dp", "mp", None), P("dp", None, None)),
        check_vma=False,
    )
```

profile of v0, /device:TPU:1, one launch (start us, length us, event | category | flops | bytes accessed | tf_op | source)
XLA Modules:
  0.0 281.1 jit_solution(16003842988223423647)
XLA Ops:
  8.0 0.0 copy-start
  8.0 0.0 all-reduce.2.cloned.1.call-start
  8.1 4.6 %reshape.17 = bf16[1024,2,512]{2,1,0:T(2,128)(2,1)} reshape(bf16[1024,1024]{1,0:T(8,128)(2,1)} %param.8) | data formatting | bytes 4194304 | tf_op jit(solution)/shard_map/reshape | solution.py:17
  12.7 0.0 copy-done
  12.7 3.4 %fusion.6 = bf16[24,2,32,512]{3,2,0,1:T(8,128)(2,1)S(1)} fusion(bf16[24,32,1024]{2,1,0:T(8,128)(2,1)S(1)} %copy-done, bf16[1024,2,512,1]{2,1,0,3:T(2,128)(2,1)} %bitcast.16), kind=kOutput, calls=%fused_computation.5 | convolution fusion | flops 1611399168 | bytes 5242880 | tf_op jit(solution)/shard_map/irt,tjc->ijrc/dot_general | solution.py:20
  16.1 1.2 copy.13
  17.3 0.0 copy-start.6
  17.3 0.0 copy-start.5
  17.3 0.0 all-reduce.2.cloned.1.call-update
  17.3 0.0 copy-start.3
  17.3 0.0 all-gather.6.cloned.1.call-start
  17.4 0.5 all-gather.6.cloned.1.call-update
  17.9 0.0 all-gather.4.cloned.1.call-start
  18.0 0.0 copy-done.6
  18.0 0.1 compare_and_fusion
  18.1 163.1 %all-reduce.2.cloned.1.call-done = bf16[48,32,512]{2,1,0:T(8,128)(2,1)} async-done(((bf16[48,32,512]{2,1,0:T(8,128)(2,1)}), bf16[48,32,512]{2,1,0:T(8,128)(2,1)}) %all-reduce.2.cloned.1.call-update) | async-done | bytes 1572880 | tf_op jit(solution)/shard_map/psum | solution.py:24
  181.2 2.0 gather_fusion
  183.2 0.7 select_convert_fusion
  183.9 0.0 all-gather.4.cloned.1.call-update
  183.9 0.0 copy-start.2
  183.9 0.0 copy-start.4
  183.9 0.0 all-gather.8.cloned.1.call-start
  184.0 0.0 all-gather.6.cloned.1.call-done
  184.0 44.1 %all-gather.4.cloned.1.call-done = bf16[2,512,512]{2,1,0:T(8,128)(2,1)} async-done(((bf16[2,32,512]{2,1,0:T(8,128)(2,1)}), bf16[2,512,512]{2,1,0:T(8,128)(2,1)}) %all-gather.4.cloned.1.call-update) | async-done | bytes 1048592 | tf_op jit(solution)/shard_map/all_gather | solution.py:30
  228.1 0.0 copy-done.5
  228.1 0.0 copy-start.1
  228.1 2.7 convolution_convert_fusion.1
  230.8 0.0 all-gather.8.cloned.1.call-update
  230.8 0.0 copy-done.3
  230.8 0.0 copy-done.1
  230.9 1.1 convolution_add_fusion.1
  232.0 0.0 copy-done.2
  232.0 0.0 copy-done.4
  232.0 1.1 convolution_add_fusion
  233.1 38.1 %all-gather.8.cloned.1.call-done = bf16[2,512,512]{2,1,0:T(8,128)(2,1)} async-done(((bf16[2,32,512]{2,1,0:T(8,128)(2,1)}), bf16[2,512,512]{2,1,0:T(8,128)(2,1)}) %all-gather.8.cloned.1.call-update) | async-done | bytes 1048592 | tf_op jit(solution)/shard_map/all_gather | solution.py:50
  271.2 2.3 copy.27
  (1 shorter events, 0.0 us)
Async XLA Ops:
  8.0 4.7 %copy-start = (bf16[24,32,1024]{2,1,0:T(8,128)(2,1)S(1)}, bf16[24,32,1024]{2,1,0:T(8,128)(2,1)}, u32[]{:S(2)}) copy-start(bf16[24,32,1024]{2,1,0:T(8,128)(2,1)} %param.7) | copy-start | bytes 4718596
  8.0 173.2 %all-reduce.2.cloned.1.call-start = ((), (), s32[]{:S(2)}) async-start(), calls=%async_computation | async-start | bytes 3145728 | tf_op jit(solution)/shard_map/psum | solution.py:24
  17.3 0.7 copy-start.6
  17.3 210.8 %copy-start.5 = (bf16[2,32,512]{2,1,0:T(8,128)(2,1)S(1)}, bf16[2,32,512]{2,1,0:T(8,128)(2,1)}, u32[]{:S(2)}) copy-start(bf16[2,32,512]{2,1,0:T(8,128)(2,1)} %param.12) | copy-start | bytes 196612
  17.3 213.5 %copy-start.3 = (f32[2,32,512]{2,1,0:T(8,128)S(1)}, f32[2,32,512]{2,1,0:T(8,128)}, u32[]{:S(2)}) copy-start(f32[2,32,512]{2,1,0:T(8,128)} %param.11) | copy-start | bytes 393220
  17.3 166.6 %all-gather.6.cloned.1.call-start = ((), (), s32[]{:S(2)}) async-start(), calls=%async_computation.2 | async-start | bytes 1114112 | tf_op jit(solution)/shard_map/all_gather | solution.py:47
  17.9 210.1 %all-gather.4.cloned.1.call-start = ((), (), s32[]{:S(2)}) async-start(), calls=%async_computation.1 | async-start | bytes 1114112 | tf_op jit(solution)/shard_map/all_gather | solution.py:30
  183.9 48.1 %copy-start.2 = (bf16[2,32,512]{2,1,0:T(8,128)(2,1)S(1)}, bf16[2,32,512]{2,1,0:T(8,128)(2,1)}, u32[]{:S(2)}) copy-start(bf16[2,32,512]{2,1,0:T(8,128)(2,1)} %select_convert_fusion) | copy-start | bytes 196612
  183.9 48.1 %copy-start.4 = (f32[2,32,512]{2,1,0:T(8,128)S(1)}, f32[2,32,512]{2,1,0:T(8,128)}, u32[]{:S(2)}) copy-start(f32[2,32,512]{2,1,0:T(8,128)} %param.10) | copy-start | bytes 393220
  183.9 87.3 %all-gather.8.cloned.1.call-start = ((), (), s32[]{:S(2)}) async-start(), calls=%async_computation.3 | async-start | bytes 1114112 | tf_op jit(solution)/shard_map/all_gather | solution.py:50
  228.1 2.8 copy-start.1
Sparse Core Ops, SparseCore 0:
  17.5 163.6 all-reduce.1
Sparse Core Ops, SparseCore 1:
  20.2 48.1 all-gather.5
  184.0 44.0 all-gather.3
  230.9 40.2 all-gather.7
where the time goes:
time: 281 us
  waiting for transfers between devices  246 us (88%)
  between operations  15.8 us (6%)
  local copies, waits for them, and re-layouts  10.1 us (4%)
  matrix products  8.31 us (3%)
    psum x1, waiting for transfers between devices, local(): lax.psum(partial_grad.astype(jnp.bfloat16), 'dp').astype(jnp.float32)  163 us
    all_gather x1, waiting for transfers between devices, local(): shard_piece = lax.all_gather(grad_b, 'mp', axis=1, tiled=True)  44.1 us
    all_gather x1, waiting for transfers between devices, local(): lax.all_gather(right_applied.astype(jnp.bfloat16), 'mp', axis=1, tiled=True)  38.1 us
  transfers between devices with their start and end apart: 4, of which 3 were waited for; matrix products, arithmetic and copies ran while one was open for 2% of the time, Pallas kernels for 0%

commit v1 on v0

v1 whole, which is shorter than its diff:
```python
import jax
import jax.numpy as jnp
from jax import lax
from jax.experimental import pallas as pl
from jax.experimental.pallas import tpu as pltpu
from jax.sharding import Mesh, PartitionSpec as P

NY, NX, NZ, NC = 8, 4, 8, 2
ROW_BLOCKS, COL_BLOCKS, SLOTS = 24, 2, 2
BLOCKS = ROW_BLOCKS * COL_BLOCKS
ROWS, WIDTH = 32, 512
DECAY = 0.95
STEPS = 4
bf16, f32 = jnp.bfloat16, jnp.float32


def partial_kernel(slots, act, cot, out, blocks):
    step = pl.program_id(0)
    per = ROW_BLOCKS // STEPS
    a = act[...].reshape(per * ROWS, act.shape[2])
    for j in range(COL_BLOCKS):
        part = jnp.dot(a, cot[:, j * WIDTH:(j + 1) * WIDTH], preferred_element_type=f32)
        part = part.astype(bf16).reshape(per, ROWS, WIDTH)
        for i in range(per):
            blocks[(step * per + i) * COL_BLOCKS + j] = part[i]

    @pl.when(step == STEPS - 1)
    def _():
        for x in range(NX):
            for y in range(NY):
                for t in range(SLOTS):
                    b = slots[(y * NX + x) * SLOTS + t]
                    at = (x * NY + y) * SLOTS + t
                    piece = blocks[jnp.minimum(b, BLOCKS - 1)]
                    out[at] = jnp.where(b < BLOCKS, piece, jnp.zeros_like(piece))


def packed_partials(slot_blocks, activations, cotangent):
    tokens = cotangent.shape[0]
    per = ROW_BLOCKS // STEPS
    total = NX * NY * SLOTS
    return pl.pallas_call(
        partial_kernel,
        grid_spec=pltpu.PrefetchScalarGridSpec(
            num_scalar_prefetch=1,
            grid=(STEPS,),
            in_specs=[
                pl.BlockSpec((per, ROWS, tokens), lambda i, s: (i, 0, 0)),
                pl.BlockSpec((tokens, COL_BLOCKS * WIDTH), lambda i, s: (0, 0)),
            ],
            out_specs=pl.BlockSpec((total, ROWS, WIDTH), lambda i, s: (0, 0, 0)),
            scratch_shapes=[pltpu.VMEM((BLOCKS, ROWS, WIDTH), bf16)],
        ),
        out_shape=jax.ShapeDtypeStruct((total, ROWS, WIDTH), bf16),
        compiler_params=pltpu.CompilerParams(vmem_limit_bytes=32 * 2**20),
        cost_estimate=pl.CostEstimate(
            flops=2 * ROW_BLOCKS * ROWS * tokens * COL_BLOCKS * WIDTH, bytes_accessed=6 * 2**20, transcendentals=0
        ),
    )(slot_blocks, activations, cotangent)


def final_kernel(place, g_own, g_other, w_own, w_other, left_stat, right_stat, left_new, right_new, precond, g, w):
    core, me = place[0], place[1]

    def rows(z, c):
        return pl.ds(pl.multiple_of((z * NC + c) * ROWS, ROWS), ROWS)

    for z in range(NZ):
        for s in range(SLOTS):
            g[s, rows(z, core), :] = g_own[z, s]
            g[s, rows(z, 1 - core), :] = g_other[z, s]
            for k in range(2):
                w[k, s, rows(z, core), :] = w_own[z, k, s]
                w[k, s, rows(z, 1 - core), :] = w_other[z, k, s]

    mine = pl.ds(pl.multiple_of(me * ROWS, ROWS), ROWS)
    row_id = lax.broadcasted_iota(jnp.int32, (ROWS, WIDTH), 0) + me * ROWS
    col_id = lax.broadcasted_iota(jnp.int32, (ROWS, WIDTH), 1)
    pick = jnp.where(row_id == col_id, 1.0, 0.0).astype(bf16)
    for s in range(SLOTS):
        grad = g[s]
        both = jnp.concatenate([g[s, mine, :], pick], axis=0)
        wide = lax.dot_general(both, grad, (((1,), (1,)), ((), ())), preferred_element_type=f32)
        left_new[s] = DECAY * left_stat[s] + wide[:ROWS]
        own_cols = wide[ROWS:].astype(bf16)
        right_new[s] = DECAY * right_stat[s] + jnp.dot(own_cols, grad, preferred_element_type=f32)
        lifted = jnp.dot(w[0, s], grad, preferred_element_type=f32).astype(bf16)
        precond[s] = jnp.dot(lifted, w[1, s], preferred_element_type=f32).astype(bf16)


def final(place, g_own, g_other, w_own, w_other, left_stat, right_stat):
    vmem = pl.BlockSpec(memory_space=pltpu.VMEM)
    full = (SLOTS, NZ * NC * ROWS, WIDTH)
    return pl.pallas_call(
        final_kernel,
        in_specs=[pl.BlockSpec(memory_space=pltpu.SMEM)] + [vmem] * 6,
        out_specs=(vmem, vmem, vmem),
        out_shape=(
            jax.ShapeDtypeStruct(left_stat.shape, f32),
            jax.ShapeDtypeStruct(right_stat.shape, f32),
            jax.ShapeDtypeStruct(full, bf16),
        ),
        scratch_shapes=[pltpu.VMEM(full, bf16), pltpu.VMEM((2,) + full, bf16)],
        compiler_params=pltpu.CompilerParams(vmem_limit_bytes=40 * 2**20),
        cost_estimate=pl.CostEstimate(flops=12 * 10**8, bytes_accessed=8 * 2**20, transcendentals=0),
    )(place, g_own, g_other, w_own, w_other, left_stat, right_stat)


def spread(piece):
    own = lax.all_to_all(jnp.broadcast_to(piece[None], (NZ,) + piece.shape), "z", 0, 0, tiled=True)
    return own, lax.ppermute(own, "core", [(0, 1), (1, 0)])


def local(activations, cotangent, slot_blocks, left_stat, right_stat, left_root, right_root):
    w_own, w_other = spread(jnp.stack([left_root, right_root]))
    packed = packed_partials(slot_blocks, activations, cotangent)
    got = lax.all_to_all(packed.reshape(NX, NY * SLOTS, ROWS, WIDTH), "x", 0, 0, tiled=True)
    over_x = jnp.sum(got.astype(f32), axis=0).astype(bf16)
    got = lax.all_to_all(over_x.reshape(NY, SLOTS, ROWS, WIDTH), "y", 0, 0, tiled=True)
    grad_b = jnp.sum(got.astype(f32), axis=0).astype(bf16)
    g_own, g_other = spread(grad_b)
    core = lax.axis_index("core")
    place = jnp.stack([core, lax.axis_index("z") * NC + core]).astype(jnp.int32)
    return final(place, g_own, g_other, w_own, w_other, left_stat, right_stat)


def solution(mesh):
    grid = Mesh(mesh.devices.reshape(NY, NX, NZ, NC), ("y", "x", "z", "core"))
    dp, mp = ("y", "x"), ("z", "core")
    return jax.shard_map(
        local,
        mesh=grid,
        in_specs=(P(None, mp, dp), P(dp, None), P(), P(dp, mp, None), P(dp, mp, None), P(dp, mp, None), P(dp, mp, None)),
        out_specs=(P(dp, mp, None), P(dp, mp, None), P(dp, None, None)),
        check_vma=False,
    )
```

time: 281 us -> 129 us (0.46)
  waiting for transfers between devices: 246 us -> 53.3 us
  starting transfers between devices: 0.17 us -> 34.9 us
  blocking collectives: 0 us -> 26.3 us
  between operations: 15.8 us -> 0.71 us
  matrix products: 8.31 us -> 0 us
  Pallas kernels: 0 us -> 6.73 us
  local copies, waits for them, and re-layouts: 10.1 us -> 5.59 us
    psum x1 -> x0, waiting for transfers between devices: 163 us -> none  [local(): lax.psum(partial_grad.astype(jnp.bfloat16), 'dp').astype(jnp.float32)]
    all_gather x3 -> x0, waiting for transfers between devices: 82.2 us -> none  [the longest x1 44.1 us: local(): shard_piece = lax.all_gather(grad_b, 'mp', axis=1, tiled=True)]
    all_to_all x0 -> x3, waiting for transfers between devices: none -> 51.8 us  [the longest x2 36.3 us: spread(): lax.all_to_all(jnp.broadcast_to(piece[None], (NZ,) + piece.shape), 'z', 0...]
    all_to_all x0 -> x1, blocking collectives: none -> 26.3 us  [local(): lax.all_to_all(packed.reshape(NX, NY * SLOTS, ROWS, WIDTH), 'x', 0, 0, ti...]
    all_to_all x0 -> x3, starting transfers between devices: none -> 24.2 us  [the longest x2 13.7 us: spread(): lax.all_to_all(jnp.broadcast_to(piece[None], (NZ,) + piece.shape), 'z', 0...]
    ppermute x0 -> x2, starting transfers between devices: none -> 10.7 us  [spread(): return (own, lax.ppermute(own, 'core', [(0, 1), (1, 0)]))]
    dot_general x4 -> x0, matrix products: 8.31 us -> none  [the longest x1 3.38 us: local(): jnp.einsum('irt,tjc->ijrc', activations, cot_blocks, preferred_element_ty...]
    pallas_call x0 -> x2, Pallas kernels: none -> 6.73 us  [the longest x1 3.51 us: final(): pl.pallas_call(final_kernel, in_specs=[pl.BlockSpec(memory_space=pltpu.SM...]
  transfers between devices with their start and end apart: 4 -> 5, of which waited for: 3 -> 4; matrix products, arithmetic and copies ran while one was open for 2% -> 0% of each run, Pallas kernels for 0% -> 0%
where the time goes in v1:
time: 129 us
  waiting for transfers between devices  53.3 us (41%)
  starting transfers between devices  34.9 us (27%)
  blocking collectives  26.3 us (20%)
  Pallas kernels  6.73 us (5%)
  local copies, waits for them, and re-layouts  5.59 us (4%)
  other arithmetic  1.49 us (1%)
    all_to_all x2, waiting for transfers between devices, spread(): lax.all_to_all(jnp.broadcast_to(piece[None], (NZ,) + piece.shape), 'z', 0...  36.3 us
    all_to_all x1, blocking collectives, local(): lax.all_to_all(packed.reshape(NX, NY * SLOTS, ROWS, WIDTH), 'x', 0, 0, ti...  26.3 us
    all_to_all x1, waiting for transfers between devices, local(): lax.all_to_all(over_x.reshape(NY, SLOTS, ROWS, WIDTH), 'y', 0, 0, tiled=T...  15.5 us
    all_to_all x2, starting transfers between devices, spread(): lax.all_to_all(jnp.broadcast_to(piece[None], (NZ,) + piece.shape), 'z', 0...  13.7 us
    ppermute x2, starting transfers between devices, spread(): return (own, lax.ppermute(own, 'core', [(0, 1), (1, 0)]))  10.7 us
    all_to_all x1, starting transfers between devices, local(): lax.all_to_all(over_x.reshape(NY, SLOTS, ROWS, WIDTH), 'y', 0, 0, tiled=T...  10.6 us
    unnamed x14, local copies, waits for them, and re-layouts  3.66 us
    pallas_call x1, Pallas kernels, final(): pl.pallas_call(final_kernel, in_specs=[pl.BlockSpec(memory_space=pltpu.SM...  3.51 us
  transfers between devices with their start and end apart: 5, of which 4 were waited for; matrix products, arithmetic and copies ran while one was open for 0% of the time, Pallas kernels for 0%

profile of v1, /device:TPU:1, one launch (start us, length us, event | category | flops | bytes accessed | tf_op | source)
XLA Modules:
  0.0 129.0 jit_solution(8081936437909280230)
XLA Ops:
  0.6 0.0 copy-start
  0.6 1.6 %copy-done = bf16[1024,1024]{1,0:T(8,128)(2,1)S(1)} copy-done((bf16[1024,1024]{1,0:T(8,128)(2,1)S(1)}, bf16[1024,1024]{1,0:T(8,128)(2,1)}, u32[]{:S(2)}) %copy-start) | copy-done | bytes 2097176
  2.2 0.0 copy-start.1
  2.2 1.4 %copy-done.1 = bf16[24,32,1024]{2,1,0:T(8,128)(2,1)S(1)} copy-done((bf16[24,32,1024]{2,1,0:T(8,128)(2,1)S(1)}, bf16[24,32,1024]{2,1,0:T(8,128)(2,1)}, u32[]{:S(2)}) %copy-start.1) | copy-done | bytes 1572888
  3.6 0.0 copy-start.4
  3.6 0.7 copy-done.4
  4.3 3.2 %shard_map.94 = bf16[64,32,512]{2,1,0:T(8,128)(2,1)S(1)} custom-call(s32[64]{0:T(128)S(1)} %copy-done.4, bf16[24,32,1024]{2,1,0:T(8,128)(2,1)S(1)} %copy-done.1, bf16[1024,1024]{1,0:T(8,128)(2,1)S(1)} %copy-done), custom_call_target="tpu_custom_call" | custom-call | flops 1610612736 | bytes 6291456 | tf_op jit(solution)/shard_map/pallas_call | solution.py:42
  7.5 26.3 %all_to_all.20 = bf16[4,16,32,512]{3,2,1,0:T(8,128)(2,1)S(1)} all-to-all(bf16[4,16,32,512]{3,2,1,0:T(8,128)(2,1)S(1)} %bitcast.6), channel_id=1, replica_groups=mesh['y'=8,'x'=4,'z'=8,'core'=2] {'x'}, dimensions={0} | all-to-all | bytes 4194304 | tf_op jit(solution)/shard_map/all_to_all | solution.py:117
  33.8 0.0 copy-start.5
  33.8 0.0 copy-start.6
  33.8 1.3 %reduce_sum.24 = bf16[16,32,512]{2,1,0:T(8,128)(2,1)} reduce(bf16[4,16,32,512]{3,2,1,0:T(8,128)(2,1)S(1)} %all_to_all.20, bf16[]{:T(256)} %constant.13.clone.1), dimensions={0}, to_apply=%region_0.0 | reduce | flops 786432 | bytes 2621442 | tf_op jit(solution)/shard_map/reduce_sum | solution.py:118
  35.1 10.6 %all-to-all-start.1 = ((bf16[8,2,32,512]{3,2,1,0:T(8,128)(2,1)}), bf16[8,2,32,512]{3,2,1,0:T(8,128)(2,1)S(1)}, u32[]{:S(2)}, u32[]{:S(2)}) async-start(bf16[8,2,32,512]{3,2,1,0:T(8,128)(2,1)} %bitcast.3), calls=%async_computation.1 | async-start | bytes 1048576 | tf_op jit(solution)/shard_map/all_to_all | solution.py:119
  45.7 0.0 copy-done.5
  45.7 0.0 copy-done.6
  45.8 15.5 %all-to-all-done.1 = bf16[8,2,32,512]{3,2,1,0:T(8,128)(2,1)S(1)} async-done(((bf16[8,2,32,512]{3,2,1,0:T(8,128)(2,1)}), bf16[8,2,32,512]{3,2,1,0:T(8,128)(2,1)S(1)}, u32[]{:S(2)}, u32[]{:S(2)}) %all-to-all-start.1) | async-done | bytes 524320 | tf_op jit(solution)/shard_map/all_to_all | solution.py:119
  61.3 1.1 broadcast_in_dim.5
  62.4 0.0 copy-start.2
  62.4 0.0 copy-start.3
  62.4 10.2 %all-to-all-start.3 = ((bf16[8,2,2,32,512]{4,3,2,1,0:T(8,128)(2,1)}), bf16[8,2,2,32,512]{4,3,2,1,0:T(8,128)(2,1)S(1)}, u32[]{:S(2)}, u32[]{:S(2)}) async-start(bf16[8,2,2,32,512]{4,3,2,1,0:T(8,128)(2,1)} %broadcast_in_dim.5), calls=%async_computation.3 | async-start | bytes 2097152 | tf_op jit(solution)/shard_map/all_to_all | solution.py:110
  72.6 0.1 reduce_sum.25
  72.6 26.7 %all-to-all-done.3.w_own = bf16[8,2,2,32,512]{4,3,2,1,0:T(8,128)(2,1)S(1)} async-done(((bf16[8,2,2,32,512]{4,3,2,1,0:T(8,128)(2,1)}), bf16[8,2,2,32,512]{4,3,2,1,0:T(8,128)(2,1)S(1)}, u32[]{:S(2)}, u32[]{:S(2)}) %all-to-all-start.3) | async-done | bytes 1048608 | tf_op jit(solution)/shard_map/all_to_all | solution.py:110
  99.4 0.8 broadcast_in_dim.4
  100.2 3.5 %all-to-all-start.2 = ((bf16[8,2,32,512]{3,2,1,0:T(8,128)(2,1)}), bf16[8,2,32,512]{3,2,1,0:T(8,128)(2,1)S(1)}, u32[]{:S(2)}, u32[]{:S(2)}) async-start(bf16[8,2,32,512]{3,2,1,0:T(8,128)(2,1)} %broadcast_in_dim.4), calls=%async_computation.2 | async-start | bytes 1048576 | tf_op jit(solution)/shard_map/all_to_all | solution.py:110
  103.7 4.8 %collective-permute-start.1 = (bf16[8,2,2,32,512]{4,3,2,1,0:T(8,128)(2,1)S(1)}, bf16[8,2,2,32,512]{4,3,2,1,0:T(8,128)(2,1)S(1)}, u32[]{:S(2)}, u32[]{:S(2)}) collective-permute-start(bf16[8,2,2,32,512]{4,3,2,1,0:T(8,128)(2,1)S(1)} %all-to-all-done.3.w_own), channel_id=1, source_target_pairs={{0,1},{1,0},{2,3},{3,2},{4,5},{5,4},{6,7},{7,6},{8,9},{9,8},{10,11... | collective-permute-start | bytes 3145736 | tf_op jit(solution)/shard_map/ppermute | solution.py:111
  108.6 9.5 %all-to-all-done.2.g_own = bf16[8,2,32,512]{3,2,1,0:T(8,128)(2,1)S(1)} async-done(((bf16[8,2,32,512]{3,2,1,0:T(8,128)(2,1)}), bf16[8,2,32,512]{3,2,1,0:T(8,128)(2,1)S(1)}, u32[]{:S(2)}, u32[]{:S(2)}) %all-to-all-start.2) | async-done | bytes 524320 | tf_op jit(solution)/shard_map/all_to_all | solution.py:110
  118.1 5.9 %collective-permute-start = (bf16[8,2,32,512]{3,2,1,0:T(8,128)(2,1)S(1)}, bf16[8,2,32,512]{3,2,1,0:T(8,128)(2,1)S(1)}, u32[]{:S(2)}, u32[]{:S(2)}) collective-permute-start(bf16[8,2,32,512]{3,2,1,0:T(8,128)(2,1)S(1)} %all-to-all-done.2.g_own), channel_id=1, source_target_pairs={{0,1},{1,0},{2,3},{3,2},{4,5},{5,4},{6,7},{7,6},{8,9},{9,8},{10,11... | collective-permute-start | bytes 1572872 | tf_op jit(solution)/shard_map/ppermute | solution.py:111
  124.0 0.1 pad_add_fusion.place
  124.1 0.0 collective-permute-done.1.w_other
  124.1 1.4 %collective-permute-done.g_other = bf16[8,2,32,512]{3,2,1,0:T(8,128)(2,1)S(1)} collective-permute-done((bf16[8,2,32,512]{3,2,1,0:T(8,128)(2,1)S(1)}, bf16[8,2,32,512]{3,2,1,0:T(8,128)(2,1)S(1)}, u32[]{:S(2)}, u32[]{:S(2)}) %collective-permute-start) | collective-permute-done | bytes 524320 | tf_op jit(solution)/shard_map/ppermute | solution.py:111
  125.5 0.0 copy-done.2
  125.5 0.0 copy-done.3
  125.5 3.5 %shard_map.95 = (f32[2,32,512]{2,1,0:T(8,128)}, f32[2,32,512]{2,1,0:T(8,128)}, bf16[2,512,512]{2,1,0:T(8,128)(2,1)}) custom-call(s32[2]{0:T(128)S(1)} %pad_add_fusion.place, bf16[8,2,32,512]{3,2,1,0:T(8,128)(2,1)S(1)} %all-to-all-done.2.g_own, bf16[8,2,32,512]{3,2,1,0:T(8,128)(2,1)S(1)} %collective-permute-done.g_other, ...), custom_call_target="tpu_custom_call" | custom-call | flops 1200000000 | bytes 8388608 | tf_op jit(solution)/shard_map/pallas_call | solution.py:94
  (1 shorter events, 0.0 us)
Async XLA Ops:
  0.6 1.6 %copy-start = (bf16[1024,1024]{1,0:T(8,128)(2,1)S(1)}, bf16[1024,1024]{1,0:T(8,128)(2,1)}, u32[]{:S(2)}) copy-start(bf16[1024,1024]{1,0:T(8,128)(2,1)} %cot.1) | copy-start | bytes 6291460
  2.2 1.4 %copy-start.1 = (bf16[24,32,1024]{2,1,0:T(8,128)(2,1)S(1)}, bf16[24,32,1024]{2,1,0:T(8,128)(2,1)}, u32[]{:S(2)}) copy-start(bf16[24,32,1024]{2,1,0:T(8,128)(2,1)} %act.1) | copy-start | bytes 4718596
  3.6 0.7 copy-start.4
  33.8 11.9 %copy-start.5 = (bf16[2,32,512]{2,1,0:T(8,128)(2,1)S(1)}, bf16[2,32,512]{2,1,0:T(8,128)(2,1)}, u32[]{:S(2)}) copy-start(bf16[2,32,512]{2,1,0:T(8,128)(2,1)} %param.13) | copy-start | bytes 196612
  33.8 11.9 %copy-start.6 = (bf16[2,32,512]{2,1,0:T(8,128)(2,1)S(1)}, bf16[2,32,512]{2,1,0:T(8,128)(2,1)}, u32[]{:S(2)}) copy-start(bf16[2,32,512]{2,1,0:T(8,128)(2,1)} %param.12) | copy-start | bytes 196612
  35.1 26.2 %all-to-all-start.1 = ((bf16[8,2,32,512]{3,2,1,0:T(8,128)(2,1)}), bf16[8,2,32,512]{3,2,1,0:T(8,128)(2,1)S(1)}, u32[]{:S(2)}, u32[]{:S(2)}) async-start(bf16[8,2,32,512]{3,2,1,0:T(8,128)(2,1)} %bitcast.3), calls=%async_computation.1 | async-start | bytes 1048576 | tf_op jit(solution)/shard_map/all_to_all | solution.py:119
  62.4 63.1 %copy-start.2 = (f32[2,32,512]{2,1,0:T(8,128)S(1)}, f32[2,32,512]{2,1,0:T(8,128)}, u32[]{:S(2)}) copy-start(f32[2,32,512]{2,1,0:T(8,128)} %left_stat.1) | copy-start | bytes 393220
  62.4 63.1 %copy-start.3 = (f32[2,32,512]{2,1,0:T(8,128)S(1)}, f32[2,32,512]{2,1,0:T(8,128)}, u32[]{:S(2)}) copy-start(f32[2,32,512]{2,1,0:T(8,128)} %right_stat.1) | copy-start | bytes 393220
  62.4 37.0 %all-to-all-start.3 = ((bf16[8,2,2,32,512]{4,3,2,1,0:T(8,128)(2,1)}), bf16[8,2,2,32,512]{4,3,2,1,0:T(8,128)(2,1)S(1)}, u32[]{:S(2)}, u32[]{:S(2)}) async-start(bf16[8,2,2,32,512]{4,3,2,1,0:T(8,128)(2,1)} %broadcast_in_dim.5), calls=%async_computation.3 | async-start | bytes 2097152 | tf_op jit(solution)/shard_map/all_to_all | solution.py:110
  100.2 17.9 %all-to-all-start.2 = ((bf16[8,2,32,512]{3,2,1,0:T(8,128)(2,1)}), bf16[8,2,32,512]{3,2,1,0:T(8,128)(2,1)S(1)}, u32[]{:S(2)}, u32[]{:S(2)}) async-start(bf16[8,2,32,512]{3,2,1,0:T(8,128)(2,1)} %broadcast_in_dim.4), calls=%async_computation.2 | async-start | bytes 1048576 | tf_op jit(solution)/shard_map/all_to_all | solution.py:110
  103.7 20.4 %collective-permute-start.1 = (bf16[8,2,2,32,512]{4,3,2,1,0:T(8,128)(2,1)S(1)}, bf16[8,2,2,32,512]{4,3,2,1,0:T(8,128)(2,1)S(1)}, u32[]{:S(2)}, u32[]{:S(2)}) collective-permute-start(bf16[8,2,2,32,512]{4,3,2,1,0:T(8,128)(2,1)S(1)} %all-to-all-done.3.w_own), channel_id=1, source_target_pairs={{0,1},{1,0},{2,3},{3,2},{4,5},{5,4},{6,7},{7,6},{8,9},{9,8},{10,11... | collective-permute-start | bytes 3145736 | tf_op jit(solution)/shard_map/ppermute | solution.py:111
  118.1 7.4 %collective-permute-start = (bf16[8,2,32,512]{3,2,1,0:T(8,128)(2,1)S(1)}, bf16[8,2,32,512]{3,2,1,0:T(8,128)(2,1)S(1)}, u32[]{:S(2)}, u32[]{:S(2)}) collective-permute-start(bf16[8,2,32,512]{3,2,1,0:T(8,128)(2,1)S(1)} %all-to-all-done.2.g_own), channel_id=1, source_target_pairs={{0,1},{1,0},{2,3},{3,2},{4,5},{5,4},{6,7},{7,6},{8,9},{9,8},{10,11... | collective-permute-start | bytes 1572872 | tf_op jit(solution)/shard_map/ppermute | solution.py:111

commit v2 on v1

v2 whole, which is shorter than its diff:
```python
import jax
import jax.numpy as jnp
from jax import lax
from jax.experimental import pallas as pl
from jax.experimental.pallas import tpu as pltpu
from jax.sharding import Mesh, PartitionSpec as P

NYH, NYL, NX, NZ, NC = 4, 2, 4, 8, 2
NEAR = NYL * NX
ROW_BLOCKS, COL_BLOCKS, SLOTS = 24, 2, 2
BLOCKS = ROW_BLOCKS * COL_BLOCKS
ROWS, WIDTH = 32, 512
PARTS = 2
DECAY = 0.95
bf16, f32 = jnp.bfloat16, jnp.float32
MIB = 2**20
VMEM = pl.BlockSpec(memory_space=pltpu.VMEM)
HBM = pl.BlockSpec(memory_space=pltpu.HBM)
SMEM = pl.BlockSpec(memory_space=pltpu.SMEM)


def params(mib):
    return pltpu.CompilerParams(vmem_limit_bytes=mib * MIB)


def cost(flops, size):
    return pl.CostEstimate(flops=flops, bytes_accessed=size, transcendentals=0)


def partial_kernel(slots, act, cot, out, act_v, cot_v, blocks, nothing, act_sem, cot_sem, out_sem):
    tokens = act_v.shape[2]
    per = ROW_BLOCKS // PARTS

    def act_copy(p):
        rows = pl.ds(p * per, per)
        return pltpu.make_async_copy(act.at[rows], act_v.at[rows], act_sem.at[p])

    def cot_copy(j):
        cols = pl.ds(j * WIDTH, WIDTH)
        return pltpu.make_async_copy(cot.at[:, cols], cot_v.at[:, cols], cot_sem.at[j])

    cot_copy(0).start()
    for p in range(PARTS):
        act_copy(p).start()
    for j in range(1, COL_BLOCKS):
        cot_copy(j).start()
    nothing[...] = jnp.zeros_like(nothing)
    for j in range(COL_BLOCKS):
        cot_copy(j).wait()
        for p in range(PARTS):
            if j == 0:
                act_copy(p).wait()
            a = act_v[p * per:(p + 1) * per].reshape(per * ROWS, tokens)
            part = jnp.dot(a, cot_v[:, j * WIDTH:(j + 1) * WIDTH], preferred_element_type=f32)
            part = part.astype(bf16).reshape(per, ROWS, WIDTH)
            for i in range(per):
                blocks[(p * per + i) * COL_BLOCKS + j] = part[i]
        for yh in range(NYH):
            for near in range(NEAR):
                for t in range(SLOTS):
                    b = slots[(yh * NEAR + near) * SLOTS + t]
                    at = (near * NYH + yh) * SLOTS + t

                    @pl.when((b < BLOCKS) & (lax.rem(b, COL_BLOCKS) == j))
                    def _():
                        pltpu.make_async_copy(blocks.at[b], out.at[at], out_sem).start()

                    if j == 0:
                        @pl.when(b >= BLOCKS)
                        def _():
                            pltpu.make_async_copy(nothing, out.at[at], out_sem).start()
    pltpu.make_async_copy(out, out, out_sem).wait()


def packed_partials(slot_blocks, activations, cotangent):
    shape = (NEAR * NYH * SLOTS, ROWS, WIDTH)
    return pl.pallas_call(
        partial_kernel,
        in_specs=[SMEM, HBM, HBM],
        out_specs=HBM,
        out_shape=jax.ShapeDtypeStruct(shape, bf16),
        scratch_shapes=[
            pltpu.VMEM(activations.shape, bf16),
            pltpu.VMEM(cotangent.shape, bf16),
            pltpu.VMEM((BLOCKS, ROWS, WIDTH), bf16),
            pltpu.VMEM((ROWS, WIDTH), bf16),
            pltpu.SemaphoreType.DMA((PARTS,)),
            pltpu.SemaphoreType.DMA((COL_BLOCKS,)),
            pltpu.SemaphoreType.DMA,
        ],
        compiler_params=params(62),
        cost_estimate=cost(2 * activations.size * cotangent.shape[1], 6 * MIB),
    )(slot_blocks, activations, cotangent)


def near_sum_kernel(got, out):
    for at in range(NYH * SLOTS):
        total = got[0, at].astype(f32)
        for n in range(1, NEAR):
            total += got[n, at].astype(f32)
        out[at] = total.astype(bf16)


def near_sum(got):
    return pl.pallas_call(
        near_sum_kernel,
        in_specs=[VMEM],
        out_specs=VMEM,
        out_shape=jax.ShapeDtypeStruct(got.shape[1:], bf16),
        compiler_params=params(16),
        cost_estimate=cost(got.size, 3 * MIB),
    )(got)


def last_sum_kernel(got, out):
    for t in range(SLOTS):
        total = got[0, t].astype(f32)
        for n in range(1, NYH):
            total += got[n, t].astype(f32)
        total = total.astype(bf16)
        for z in range(NZ):
            out[z, t] = total


def last_sum(got):
    return pl.pallas_call(
        last_sum_kernel,
        in_specs=[VMEM],
        out_specs=VMEM,
        out_shape=jax.ShapeDtypeStruct((NZ,) + got.shape[1:], bf16),
        compiler_params=params(8),
        cost_estimate=cost(got.size, MIB),
    )(got)


def rows_of(z, core):
    return pl.ds(pl.multiple_of((z * NC + core) * ROWS, ROWS), ROWS)


def roots_kernel(place, here, far, own, other, w):
    core, z_here = place[0], place[1]
    toward = 1 - 2 * core

    def put(pair, z, first):
        for s in range(SLOTS):
            for k in range(2):
                w[k, s, rows_of(z, first), :] = pair[0, k, s]
                w[k, s, rows_of(z, 1 - first), :] = pair[1, k, s]

    put(here, z_here, core)
    put(far, lax.rem(z_here + NZ // 2, NZ), core)
    for n in range(NZ // 2 - 1):
        by = (n + 1) * toward
        put(own.at[n], lax.rem(z_here - by + NZ, NZ), core)
        put(other.at[n], lax.rem(z_here + by + NZ, NZ), 1 - core)


def whole_roots(place, here, far, own, other):
    return pl.pallas_call(
        roots_kernel,
        in_specs=[SMEM] + [VMEM] * 4,
        out_specs=VMEM,
        out_shape=jax.ShapeDtypeStruct((2, SLOTS, NZ * NC * ROWS, WIDTH), bf16),
        compiler_params=params(16),
        cost_estimate=cost(0, 4 * MIB),
    )(place, here, far, own, other)


def final_kernel(place, g_own, g_other, w, left_stat, right_stat, left_new, right_new, precond, g):
    core, z_here = place[0], place[1]
    for z in range(NZ):
        for s in range(SLOTS):
            g[s, rows_of(z, core), :] = g_own[z, s]
            g[s, rows_of(z, 1 - core), :] = g_other[z, s]
    row_id = lax.broadcasted_iota(jnp.int32, (ROWS, WIDTH), 0) + (z_here * NC + core) * ROWS
    col_id = lax.broadcasted_iota(jnp.int32, (ROWS, WIDTH), 1)
    pick = jnp.where(row_id == col_id, 1.0, 0.0).astype(bf16)
    for s in range(SLOTS):
        grad = g[s]
        both = jnp.concatenate([g[s, rows_of(z_here, core), :], pick], axis=0)
        wide = lax.dot_general(both, grad, (((1,), (1,)), ((), ())), preferred_element_type=f32)
        left_new[s] = DECAY * left_stat[s] + wide[:ROWS]
        own_cols = wide[ROWS:].astype(bf16)
        right_new[s] = DECAY * right_stat[s] + jnp.dot(own_cols, grad, preferred_element_type=f32)
        lifted = jnp.dot(w[0, s], grad, preferred_element_type=f32).astype(bf16)
        precond[s] = jnp.dot(lifted, w[1, s], preferred_element_type=f32).astype(bf16)


def final(place, g_own, g_other, w, left_stat, right_stat):
    full = (SLOTS, NZ * NC * ROWS, WIDTH)
    return pl.pallas_call(
        final_kernel,
        in_specs=[SMEM] + [VMEM] * 5,
        out_specs=(VMEM, VMEM, VMEM),
        out_shape=(
            jax.ShapeDtypeStruct(left_stat.shape, f32),
            jax.ShapeDtypeStruct(right_stat.shape, f32),
            jax.ShapeDtypeStruct(full, bf16),
        ),
        scratch_shapes=[pltpu.VMEM(full, bf16)],
        compiler_params=params(32),
        cost_estimate=cost(12 * 10**8, 8 * MIB),
    )(place, g_own, g_other, w, left_stat, right_stat)


def swap(value):
    return lax.ppermute(value, "core", [(0, 1), (1, 0)])


def jump(value, by):
    pairs = []
    for z in range(NZ):
        for core in range(NC):
            pairs.append((z * NC + core, (z + by * (1 - 2 * core)) % NZ * NC + core))
    return lax.ppermute(value, ("z", "core"), pairs)


def exchange(value, axes):
    return lax.all_to_all(value, axes, 0, 0, tiled=True)


def after(value, *others):
    return lax.optimization_barrier((value,) + others)


def local(activations, cotangent, slot_blocks, left_stat, right_stat, left_root, right_root):
    place = jnp.stack([lax.axis_index("core"), lax.axis_index("z")]).astype(jnp.int32)
    roots = jnp.stack([left_root, right_root])
    pair = jnp.stack([roots, swap(roots)])
    r2 = jump(pair, 2)
    r1 = jump(pair, 1)
    r3 = jump(r2, 1)
    part = packed_partials(slot_blocks, activations, cotangent)
    part = near_sum(exchange(part.reshape(NEAR, NYH * SLOTS, ROWS, WIDTH), ("yl", "x")))
    part, r1, r3 = after(part, r1, r3)
    part = last_sum(exchange(part.reshape(NYH, SLOTS, ROWS, WIDTH), "yh"))
    r4 = jump(r3, 1)
    g_own = exchange(part, "z")
    g_own, r4 = after(g_own, r4)
    own = jnp.stack([r1, r2, r3])
    other = swap(own)
    w = whole_roots(place, pair, r4, own, other)
    return final(place, g_own, swap(g_own), w, left_stat, right_stat)


def solution(mesh):
    grid = Mesh(mesh.devices.reshape(NYH, NYL, NX, NZ, NC), ("yh", "yl", "x", "z", "core"))
    dp, mp = ("yh", "yl", "x"), ("z", "core")
    return jax.shard_map(
        local,
        mesh=grid,
        in_specs=(P(None, mp, dp), P(dp, None), P(), P(dp, mp, None), P(dp, mp, None), P(dp, mp, None), P(dp, mp, None)),
        out_specs=(P(dp, mp, None), P(dp, mp, None), P(dp, None, None)),
        check_vma=False,
    )
```

time: 129 us -> 90.4 us (0.70)
  waiting for transfers between devices: 53.3 us -> 14.9 us
  starting transfers between devices: 34.9 us -> 49.3 us
  blocking collectives: 26.3 us -> 13.6 us
  local copies, waits for them, and re-layouts: 5.59 us -> 0.02 us
  Pallas kernels: 6.73 us -> 10.7 us
    all_to_all x3 -> x2, waiting for transfers between devices: 51.8 us -> 0.01 us  [exchange(): return lax.all_to_all(value, axes, 0, 0, tiled=True)]
    ppermute x2 -> x7, starting transfers between devices: 10.7 us -> 35 us  [the longest x4 18.6 us: jump(): return lax.ppermute(value, ('z', 'core'), pairs)]
    ppermute x2 -> x7, waiting for transfers between devices: 1.43 us -> 14.9 us  [the longest x4 13.2 us: jump(): return lax.ppermute(value, ('z', 'core'), pairs)]
    all_to_all x1, blocking collectives: 26.3 us -> 13.6 us  [exchange(): return lax.all_to_all(value, axes, 0, 0, tiled=True)]
    all_to_all x3 -> x2, starting transfers between devices: 24.2 us -> 14.3 us  [exchange(): return lax.all_to_all(value, axes, 0, 0, tiled=True)]
    pallas_call x2 -> x5, Pallas kernels: 6.73 us -> 10.7 us  [the longest x1 5.47 us: packed_partials(): pl.pallas_call(partial_kernel, in_specs=[SMEM, HBM, HBM], out_specs=HBM,...]
    unnamed x14 -> x8, local copies, waits for them, and re-layouts: 3.66 us -> 0.02 us
    broadcast_in_dim x2 -> x0, local copies, waits for them, and re-layouts: 1.93 us -> none  [spread(): jnp.broadcast_to(piece[None], (NZ,) + piece.shape)]
  transfers between devices with their start and end apart: 5 -> 9, of which waited for: 4 -> 5; matrix products, arithmetic and copies ran while one was open for 0% -> 0% of each run, Pallas kernels for 0% -> 1%
where the time goes in v2:
time: 90.4 us; the launch traced here: 89.6 us
  starting transfers between devices  49.3 us (55%)
  waiting for transfers between devices  14.9 us (16%)
  blocking collectives  13.6 us (15%)
  Pallas kernels  10.7 us (12%)
    ppermute x4, starting transfers between devices, jump(): return lax.ppermute(value, ('z', 'core'), pairs)  18.6 us
    ppermute x3, starting transfers between devices, swap(): return lax.ppermute(value, 'core', [(0, 1), (1, 0)])  16.4 us
    all_to_all x2, starting transfers between devices, exchange(): return lax.all_to_all(value, axes, 0, 0, tiled=True)  14.3 us
    all_to_all x1, blocking collectives, exchange(): return lax.all_to_all(value, axes, 0, 0, tiled=True)  13.6 us
    ppermute x4, waiting for transfers between devices, jump(): return lax.ppermute(value, ('z', 'core'), pairs)  13.2 us
    pallas_call x1, Pallas kernels, packed_partials(): pl.pallas_call(partial_kernel, in_specs=[SMEM, HBM, HBM], out_specs=HBM,...  5.47 us
    pallas_call x1, Pallas kernels, final(): pl.pallas_call(final_kernel, in_specs=[SMEM] + [VMEM] * 5, out_specs=(VME...  3.47 us
  transfers between devices with their start and end apart: 9, of which 5 were waited for; matrix products, arithmetic and copies ran while one was open for 0% of the time, Pallas kernels for 1%

profile of v2, /device:TPU:1, one launch (start us, length us, event | category | flops | bytes accessed | tf_op | source)
XLA Modules:
  0.0 89.6 jit_solution(10747409234128675275)
XLA Ops:
  0.6 5.5 %shard_map.94 = bf16[64,32,512]{2,1,0:T(8,128)(2,1)} custom-call(s32[64]{0:T(128)} %slots.1, bf16[24,32,1024]{2,1,0:T(8,128)(2,1)} %act.1, bf16[1024,1024]{1,0:T(8,128)(2,1)} %cot.1), custom_call_target="tpu_custom_call" | custom-call | flops 1610612736 | bytes 6291456 | tf_op jit(solution)/shard_map/pallas_call | solution.py:77
  6.1 0.0 copy-start.2
  6.1 0.0 copy-start.3
  6.1 6.0 %all-to-all-start = ((bf16[8,8,32,512]{3,2,1,0:T(8,128)(2,1)}), bf16[8,8,32,512]{3,2,1,0:T(8,128)(2,1)S(1)}, u32[]{:S(2)}, u32[]{:S(2)}) async-start(bf16[8,8,32,512]{3,2,1,0:T(8,128)(2,1)} %bitcast.13), calls=%async_computation | async-start | bytes 4194304 | tf_op jit(solution)/shard_map/all_to_all | solution.py:219
  12.1 0.0 copy-done.2
  12.1 0.0 copy-done.3
  12.2 6.5 %collective-permute-start = (bf16[2,2,32,512]{3,2,1,0:T(8,128)(2,1)S(1)}, bf16[2,2,32,512]{3,2,1,0:T(8,128)(2,1)S(1)}, u32[]{:S(2)}, u32[]{:S(2)}) collective-permute-start(bf16[2,2,32,512]{3,2,1,0:T(8,128)(2,1)S(1)} %get-tuple-element.14), channel_id=1, source_target_pairs={{0,1},{1,0},{2,3},{3,2},{4,5},{5,4},{6,7},{7,6},{8,9},{9,8},{10,11... | collective-permute-start | bytes 393224 | tf_op jit(solution)/shard_map/ppermute | solution.py:207
  18.7 1.0 %collective-permute-done = bf16[2,2,32,512]{3,2,1,0:T(8,128)(2,1)S(1)} collective-permute-done((bf16[2,2,32,512]{3,2,1,0:T(8,128)(2,1)S(1)}, bf16[2,2,32,512]{3,2,1,0:T(8,128)(2,1)S(1)}, u32[]{:S(2)}, u32[]{:S(2)}) %collective-permute-start) | collective-permute-done | bytes 131104 | tf_op jit(solution)/shard_map/ppermute | solution.py:207
  19.7 7.0 %collective-permute-start.2 = (bf16[2,2,2,32,512]{4,3,2,1,0:T(8,128)(2,1)S(1)}, bf16[2,2,2,32,512]{4,3,2,1,0:T(8,128)(2,1)S(1)}, u32[]{:S(2)}, u32[]{:S(2)}) collective-permute-start(bf16[2,2,2,32,512]{4,3,2,1,0:T(8,128)(2,1)S(1)} %pad_maximum_fusion.1.here), channel_id=1, source_target_pairs={{0,4},{1,13},{2,6},{3,15},{4,8},{5,1},{6,10},{7,3},{8,12},{9,5},{1... | collective-permute-start | bytes 786440 | tf_op jit(solution)/shard_map/ppermute | solution.py:215
  26.7 2.2 %collective-permute-start.1 = (bf16[2,2,2,32,512]{4,3,2,1,0:T(8,128)(2,1)S(1)}, bf16[2,2,2,32,512]{4,3,2,1,0:T(8,128)(2,1)S(1)}, u32[]{:S(2)}, u32[]{:S(2)}) collective-permute-start(bf16[2,2,2,32,512]{4,3,2,1,0:T(8,128)(2,1)S(1)} %pad_maximum_fusion.1.here), channel_id=1, source_target_pairs={{0,2},{1,15},{2,4},{3,1},{4,6},{5,3},{6,8},{7,5},{8,10},{9,7},{10,... | collective-permute-start | bytes 786440 | tf_op jit(solution)/shard_map/ppermute | solution.py:215
  28.9 3.9 %collective-permute-done.2 = bf16[2,2,2,32,512]{4,3,2,1,0:T(8,128)(2,1)S(1)} collective-permute-done((bf16[2,2,2,32,512]{4,3,2,1,0:T(8,128)(2,1)S(1)}, bf16[2,2,2,32,512]{4,3,2,1,0:T(8,128)(2,1)S(1)}, u32[]{:S(2)}, u32[]{:S(2)}) %collective-permute-start.2) | collective-permute-done | bytes 262176 | tf_op jit(solution)/shard_map/ppermute | solution.py:215
  32.8 4.8 %collective-permute-start.3 = (bf16[2,2,2,32,512]{4,3,2,1,0:T(8,128)(2,1)S(1)}, bf16[2,2,2,32,512]{4,3,2,1,0:T(8,128)(2,1)S(1)}, u32[]{:S(2)}, u32[]{:S(2)}) collective-permute-start(bf16[2,2,2,32,512]{4,3,2,1,0:T(8,128)(2,1)S(1)} %collective-permute-done.2), channel_id=1, source_target_pairs={{0,2},{1,15},{2,4},{3,1},{4,6},{5,3},{6,8},{7,5},{8,10},{9,7},{10,... | collective-permute-start | bytes 786440 | tf_op jit(solution)/shard_map/ppermute | solution.py:215
  37.7 0.0 all-to-all-done.got
  37.7 0.3 shard_map.95
  38.0 0.0 collective-permute-done.1
  38.0 3.0 %collective-permute-done.3 = bf16[2,2,2,32,512]{4,3,2,1,0:T(8,128)(2,1)S(1)} collective-permute-done((bf16[2,2,2,32,512]{4,3,2,1,0:T(8,128)(2,1)S(1)}, bf16[2,2,2,32,512]{4,3,2,1,0:T(8,128)(2,1)S(1)}, u32[]{:S(2)}, u32[]{:S(2)}) %collective-permute-start.3) | collective-permute-done | bytes 262176 | tf_op jit(solution)/shard_map/ppermute | solution.py:215
  41.0 13.6 %all_to_all.15.got = bf16[4,2,32,512]{3,2,1,0:T(8,128)(2,1)S(1)} all-to-all(bf16[4,2,32,512]{3,2,1,0:T(8,128)(2,1)S(1)} %bitcast.12), channel_id=1, replica_groups=mesh['yh'=4,'yl'=2,'x'=4,'z'=8,'core'=2] {'yh'}, dimensions={0} | all-to-all | bytes 524288 | tf_op jit(solution)/shard_map/all_to_all | solution.py:219
  54.6 0.8 shard_map.96
  55.5 8.3 %all-to-all-start.2 = ((bf16[8,2,32,512]{3,2,1,0:T(8,128)(2,1)}), bf16[8,2,32,512]{3,2,1,0:T(8,128)(2,1)S(1)}, u32[]{:S(2)}, u32[]{:S(2)}) async-start(bf16[8,2,32,512]{3,2,1,0:T(8,128)(2,1)} %shard_map.96), calls=%async_computation.2 | async-start | bytes 1048576 | tf_op jit(solution)/shard_map/all_to_all | solution.py:219
  63.8 4.6 %collective-permute-start.4 = (bf16[2,2,2,32,512]{4,3,2,1,0:T(8,128)(2,1)S(1)}, bf16[2,2,2,32,512]{4,3,2,1,0:T(8,128)(2,1)S(1)}, u32[]{:S(2)}, u32[]{:S(2)}) collective-permute-start(bf16[2,2,2,32,512]{4,3,2,1,0:T(8,128)(2,1)S(1)} %collective-permute-done.3), channel_id=1, source_target_pairs={{0,2},{1,15},{2,4},{3,1},{4,6},{5,3},{6,8},{7,5},{8,10},{9,7},{10,... | collective-permute-start | bytes 786440 | tf_op jit(solution)/shard_map/ppermute | solution.py:215
  68.3 0.1 pad_maximum_fusion.own
  68.4 5.4 %collective-permute-start.6 = (bf16[3,2,2,2,32,512]{5,4,3,2,1,0:T(8,128)(2,1)S(1)}, bf16[3,2,2,2,32,512]{5,4,3,2,1,0:T(8,128)(2,1)S(1)}, u32[]{:S(2)}, u32[]{:S(2)}) collective-permute-start(bf16[3,2,2,2,32,512]{5,4,3,2,1,0:T(8,128)(2,1)S(1)} %pad_maximum_fusion.own), channel_id=1, source_target_pairs={{0,1},{1,0},{2,3},{3,2},{4,5},{5,4},{6,7},{7,6},{8,9},{9,8},{10,11... | collective-permute-start | bytes 2359304 | tf_op jit(solution)/shard_map/ppermute | solution.py:207
  73.9 6.3 %collective-permute-done.4.far = bf16[2,2,2,32,512]{4,3,2,1,0:T(8,128)(2,1)S(1)} collective-permute-done((bf16[2,2,2,32,512]{4,3,2,1,0:T(8,128)(2,1)S(1)}, bf16[2,2,2,32,512]{4,3,2,1,0:T(8,128)(2,1)S(1)}, u32[]{:S(2)}, u32[]{:S(2)}) %collective-permute-start.4) | collective-permute-done | bytes 262176 | tf_op jit(solution)/shard_map/ppermute | solution.py:215
  80.1 0.0 all-to-all-done.2.g_own
  80.1 4.5 %collective-permute-start.5 = (bf16[8,2,32,512]{3,2,1,0:T(8,128)(2,1)S(1)}, bf16[8,2,32,512]{3,2,1,0:T(8,128)(2,1)S(1)}, u32[]{:S(2)}, u32[]{:S(2)}) collective-permute-start(bf16[8,2,32,512]{3,2,1,0:T(8,128)(2,1)S(1)} %all-to-all-done.2.g_own), channel_id=1, source_target_pairs={{0,1},{1,0},{2,3},{3,2},{4,5},{5,4},{6,7},{7,6},{8,9},{9,8},{10,11... | collective-permute-start | bytes 1572872 | tf_op jit(solution)/shard_map/ppermute | solution.py:207
  84.6 0.1 pad_add_fusion.place
  84.7 0.0 copy-start
  84.7 0.0 copy-start.1
  84.7 0.0 collective-permute-done.6.other
  84.7 0.7 shard_map.97.w
  85.4 0.7 collective-permute-done.5.g_other
  86.1 0.0 copy-done
  86.2 0.0 copy-done.1
  86.2 3.5 %shard_map.98 = (f32[2,32,512]{2,1,0:T(8,128)}, f32[2,32,512]{2,1,0:T(8,128)}, bf16[2,512,512]{2,1,0:T(8,128)(2,1)}) custom-call(s32[2]{0:T(128)S(1)} %pad_add_fusion.place, bf16[8,2,32,512]{3,2,1,0:T(8,128)(2,1)S(1)} %all-to-all-done.2.g_own, bf16[8,2,32,512]{3,2,1,0:T(8,128)(2,1)S(1)} %collective-permute-done.5.g_other, ...), custom_call_target="tpu_custom_call" | custom-call | flops 1200000000 | bytes 8388608 | tf_op jit(solution)/shard_map/pallas_call | solution.py:191
  (2 shorter events, 0.0 us)
Async XLA Ops:
  6.1 6.0 %copy-start.2 = (bf16[2,32,512]{2,1,0:T(8,128)(2,1)S(1)}, bf16[2,32,512]{2,1,0:T(8,128)(2,1)}, u32[]{:S(2)}) copy-start(bf16[2,32,512]{2,1,0:T(8,128)(2,1)} %param.13) | copy-start | bytes 196612
  6.1 6.0 %copy-start.3 = (bf16[2,32,512]{2,1,0:T(8,128)(2,1)S(1)}, bf16[2,32,512]{2,1,0:T(8,128)(2,1)}, u32[]{:S(2)}) copy-start(bf16[2,32,512]{2,1,0:T(8,128)(2,1)} %param.12) | copy-start | bytes 196612
  6.1 31.5 %all-to-all-start = ((bf16[8,8,32,512]{3,2,1,0:T(8,128)(2,1)}), bf16[8,8,32,512]{3,2,1,0:T(8,128)(2,1)S(1)}, u32[]{:S(2)}, u32[]{:S(2)}) async-start(bf16[8,8,32,512]{3,2,1,0:T(8,128)(2,1)} %bitcast.13), calls=%async_computation | async-start | bytes 4194304 | tf_op jit(solution)/shard_map/all_to_all | solution.py:219
  12.2 7.5 %collective-permute-start = (bf16[2,2,32,512]{3,2,1,0:T(8,128)(2,1)S(1)}, bf16[2,2,32,512]{3,2,1,0:T(8,128)(2,1)S(1)}, u32[]{:S(2)}, u32[]{:S(2)}) collective-permute-start(bf16[2,2,32,512]{3,2,1,0:T(8,128)(2,1)S(1)} %get-tuple-element.14), channel_id=1, source_target_pairs={{0,1},{1,0},{2,3},{3,2},{4,5},{5,4},{6,7},{7,6},{8,9},{9,8},{10,11... | collective-permute-start | bytes 393224 | tf_op jit(solution)/shard_map/ppermute | solution.py:207
  19.7 13.1 %collective-permute-start.2 = (bf16[2,2,2,32,512]{4,3,2,1,0:T(8,128)(2,1)S(1)}, bf16[2,2,2,32,512]{4,3,2,1,0:T(8,128)(2,1)S(1)}, u32[]{:S(2)}, u32[]{:S(2)}) collective-permute-start(bf16[2,2,2,32,512]{4,3,2,1,0:T(8,128)(2,1)S(1)} %pad_maximum_fusion.1.here), channel_id=1, source_target_pairs={{0,4},{1,13},{2,6},{3,15},{4,8},{5,1},{6,10},{7,3},{8,12},{9,5},{1... | collective-permute-start | bytes 786440 | tf_op jit(solution)/shard_map/ppermute | solution.py:215
  26.7 11.2 %collective-permute-start.1 = (bf16[2,2,2,32,512]{4,3,2,1,0:T(8,128)(2,1)S(1)}, bf16[2,2,2,32,512]{4,3,2,1,0:T(8,128)(2,1)S(1)}, u32[]{:S(2)}, u32[]{:S(2)}) collective-permute-start(bf16[2,2,2,32,512]{4,3,2,1,0:T(8,128)(2,1)S(1)} %pad_maximum_fusion.1.here), channel_id=1, source_target_pairs={{0,2},{1,15},{2,4},{3,1},{4,6},{5,3},{6,8},{7,5},{8,10},{9,7},{10,... | collective-permute-start | bytes 786440 | tf_op jit(solution)/shard_map/ppermute | solution.py:215
  32.8 8.1 %collective-permute-start.3 = (bf16[2,2,2,32,512]{4,3,2,1,0:T(8,128)(2,1)S(1)}, bf16[2,2,2,32,512]{4,3,2,1,0:T(8,128)(2,1)S(1)}, u32[]{:S(2)}, u32[]{:S(2)}) collective-permute-start(bf16[2,2,2,32,512]{4,3,2,1,0:T(8,128)(2,1)S(1)} %collective-permute-done.2), channel_id=1, source_target_pairs={{0,2},{1,15},{2,4},{3,1},{4,6},{5,3},{6,8},{7,5},{8,10},{9,7},{10,... | collective-permute-start | bytes 786440 | tf_op jit(solution)/shard_map/ppermute | solution.py:215
  55.5 24.7 %all-to-all-start.2 = ((bf16[8,2,32,512]{3,2,1,0:T(8,128)(2,1)}), bf16[8,2,32,512]{3,2,1,0:T(8,128)(2,1)S(1)}, u32[]{:S(2)}, u32[]{:S(2)}) async-start(bf16[8,2,32,512]{3,2,1,0:T(8,128)(2,1)} %shard_map.96), calls=%async_computation.2 | async-start | bytes 1048576 | tf_op jit(solution)/shard_map/all_to_all | solution.py:219
  63.8 16.4 %collective-permute-start.4 = (bf16[2,2,2,32,512]{4,3,2,1,0:T(8,128)(2,1)S(1)}, bf16[2,2,2,32,512]{4,3,2,1,0:T(8,128)(2,1)S(1)}, u32[]{:S(2)}, u32[]{:S(2)}) collective-permute-start(bf16[2,2,2,32,512]{4,3,2,1,0:T(8,128)(2,1)S(1)} %collective-permute-done.3), channel_id=1, source_target_pairs={{0,2},{1,15},{2,4},{3,1},{4,6},{5,3},{6,8},{7,5},{8,10},{9,7},{10,... | collective-permute-start | bytes 786440 | tf_op jit(solution)/shard_map/ppermute | solution.py:215
  68.4 16.3 %collective-permute-start.6 = (bf16[3,2,2,2,32,512]{5,4,3,2,1,0:T(8,128)(2,1)S(1)}, bf16[3,2,2,2,32,512]{5,4,3,2,1,0:T(8,128)(2,1)S(1)}, u32[]{:S(2)}, u32[]{:S(2)}) collective-permute-start(bf16[3,2,2,2,32,512]{5,4,3,2,1,0:T(8,128)(2,1)S(1)} %pad_maximum_fusion.own), channel_id=1, source_target_pairs={{0,1},{1,0},{2,3},{3,2},{4,5},{5,4},{6,7},{7,6},{8,9},{9,8},{10,11... | collective-permute-start | bytes 2359304 | tf_op jit(solution)/shard_map/ppermute | solution.py:207
  80.1 6.0 %collective-permute-start.5 = (bf16[8,2,32,512]{3,2,1,0:T(8,128)(2,1)S(1)}, bf16[8,2,32,512]{3,2,1,0:T(8,128)(2,1)S(1)}, u32[]{:S(2)}, u32[]{:S(2)}) collective-permute-start(bf16[8,2,32,512]{3,2,1,0:T(8,128)(2,1)S(1)} %all-to-all-done.2.g_own), channel_id=1, source_target_pairs={{0,1},{1,0},{2,3},{3,2},{4,5},{5,4},{6,7},{7,6},{8,9},{9,8},{10,11... | collective-permute-start | bytes 1572872 | tf_op jit(solution)/shard_map/ppermute | solution.py:207
  84.7 1.4 %copy-start = (f32[2,32,512]{2,1,0:T(8,128)S(1)}, f32[2,32,512]{2,1,0:T(8,128)}, u32[]{:S(2)}) copy-start(f32[2,32,512]{2,1,0:T(8,128)} %left_stat.1) | copy-start | bytes 393220
  84.7 1.4 %copy-start.1 = (f32[2,32,512]{2,1,0:T(8,128)S(1)}, f32[2,32,512]{2,1,0:T(8,128)}, u32[]{:S(2)}) copy-start(f32[2,32,512]{2,1,0:T(8,128)} %right_stat.1) | copy-start | bytes 393220

commit v3 on v2

--- a/solution.py
+++ b/solution.py
@@ -10,6 +10,7 @@
 ROW_BLOCKS, COL_BLOCKS, SLOTS = 24, 2, 2
 BLOCKS = ROW_BLOCKS * COL_BLOCKS
 ROWS, WIDTH = 32, 512
+HALF, QUARTER = ROWS // NYL, WIDTH // NX
 PARTS = 2
 DECAY = 0.95
 bf16, f32 = jnp.bfloat16, jnp.float32
@@ -27,7 +28,7 @@
     return pl.CostEstimate(flops=flops, bytes_accessed=size, transcendentals=0)
 
 
-def partial_kernel(slots, act, cot, out, act_v, cot_v, blocks, nothing, act_sem, cot_sem, out_sem):
+def partial_kernel(act, cot, out, act_v, cot_v, cut, act_sem, cot_sem, out_sem):
     tokens = act_v.shape[2]
     per = ROW_BLOCKS // PARTS
 
@@ -38,13 +39,16 @@
     def cot_copy(j):
         cols = pl.ds(j * WIDTH, WIDTH)
         return pltpu.make_async_copy(cot.at[:, cols], cot_v.at[:, cols], cot_sem.at[j])
+
+    def out_copy(j):
+        span = pl.ds(j * ROW_BLOCKS, ROW_BLOCKS)
+        return pltpu.make_async_copy(cut.at[:, span], out.at[:, span], out_sem.at[j])
 
     cot_copy(0).start()
     for p in range(PARTS):
         act_copy(p).start()
     for j in range(1, COL_BLOCKS):
         cot_copy(j).start()
-    nothing[...] = jnp.zeros_like(nothing)
     for j in range(COL_BLOCKS):
         cot_copy(j).wait()
         for p in range(PARTS):
@@ -53,81 +57,79 @@
             a = act_v[p * per:(p + 1) * per].reshape(per * ROWS, tokens)
             part = jnp.dot(a, cot_v[:, j * WIDTH:(j + 1) * WIDTH], preferred_element_type=f32)
             part = part.astype(bf16).reshape(per, ROWS, WIDTH)
-            for i in range(per):
-                blocks[(p * per + i) * COL_BLOCKS + j] = part[i]
-        for yh in range(NYH):
-            for near in range(NEAR):
-                for t in range(SLOTS):
-                    b = slots[(yh * NEAR + near) * SLOTS + t]
-                    at = (near * NYH + yh) * SLOTS + t
-
-                    @pl.when((b < BLOCKS) & (lax.rem(b, COL_BLOCKS) == j))
-                    def _():
-                        pltpu.make_async_copy(blocks.at[b], out.at[at], out_sem).start()
-
-                    if j == 0:
-                        @pl.when(b >= BLOCKS)
-                        def _():
-                            pltpu.make_async_copy(nothing, out.at[at], out_sem).start()
-    pltpu.make_async_copy(out, out, out_sem).wait()
-
-
-def packed_partials(slot_blocks, activations, cotangent):
-    shape = (NEAR * NYH * SLOTS, ROWS, WIDTH)
+            span = slice(j * ROW_BLOCKS + p * per, j * ROW_BLOCKS + (p + 1) * per)
+            for yl in range(NYL):
+                for x in range(NX):
+                    piece = part[:, yl * HALF:(yl + 1) * HALF, x * QUARTER:(x + 1) * QUARTER]
+                    cut[yl * NX + x, span] = piece
+        out_copy(j).start()
+    for j in range(COL_BLOCKS):
+        out_copy(j).wait()
+
+
+def cut_partials(activations, cotangent):
+    shape = (NEAR, BLOCKS, HALF, QUARTER)
     return pl.pallas_call(
         partial_kernel,
-        in_specs=[SMEM, HBM, HBM],
+        in_specs=[HBM, HBM],
         out_specs=HBM,
         out_shape=jax.ShapeDtypeStruct(shape, bf16),
         scratch_shapes=[
             pltpu.VMEM(activations.shape, bf16),
             pltpu.VMEM(cotangent.shape, bf16),
-            pltpu.VMEM((BLOCKS, ROWS, WIDTH), bf16),
-            pltpu.VMEM((ROWS, WIDTH), bf16),
+            pltpu.VMEM(shape, bf16),
             pltpu.SemaphoreType.DMA((PARTS,)),
             pltpu.SemaphoreType.DMA((COL_BLOCKS,)),
-            pltpu.SemaphoreType.DMA,
+            pltpu.SemaphoreType.DMA((COL_BLOCKS,)),
         ],
         compiler_params=params(62),
         cost_estimate=cost(2 * activations.size * cotangent.shape[1], 6 * MIB),
-    )(slot_blocks, activations, cotangent)
-
-
-def near_sum_kernel(got, out):
-    for at in range(NYH * SLOTS):
-        total = got[0, at].astype(f32)
-        for n in range(1, NEAR):
-            total += got[n, at].astype(f32)
-        out[at] = total.astype(bf16)
-
-
-def near_sum(got):
+    )(activations, cotangent)
+
+
+def near_sum_kernel(blocks, got, out, total_v):
+    total = got[0].astype(f32)
+    for n in range(1, NEAR):
+        total += got[n].astype(f32)
+    total_v[:BLOCKS] = total.astype(bf16)
+    total_v[BLOCKS] = jnp.zeros((HALF, QUARTER), bf16)
+    for owner in range(NYH * NEAR):
+        for t in range(SLOTS):
+            out[owner, t] = total_v[blocks[owner * SLOTS + t]]
+
+
+def near_sum(blocks, got):
     return pl.pallas_call(
         near_sum_kernel,
-        in_specs=[VMEM],
+        in_specs=[SMEM, VMEM],
         out_specs=VMEM,
-        out_shape=jax.ShapeDtypeStruct(got.shape[1:], bf16),
+        out_shape=jax.ShapeDtypeStruct((NYH * NEAR, SLOTS, HALF, QUARTER), bf16),
+        scratch_shapes=[pltpu.VMEM((BLOCKS + 1, HALF, QUARTER), bf16)],
         compiler_params=params(16),
         cost_estimate=cost(got.size, 3 * MIB),
-    )(got)
-
-
-def last_sum_kernel(got, out):
-    for t in range(SLOTS):
-        total = got[0, t].astype(f32)
-        for n in range(1, NYH):
-            total += got[n, t].astype(f32)
-        total = total.astype(bf16)
-        for z in range(NZ):
-            out[z, t] = total
+    )(blocks, got)
+
+
+def last_sum_kernel(got, out, total_v, sem):
+    for yl in range(NYL):
+        for x in range(NX):
+            total = got[yl * NX + x].astype(f32)
+            for yh in range(1, NYH):
+                total += got[yh * NEAR + yl * NX + x].astype(f32)
+            total_v[:, yl * HALF:(yl + 1) * HALF, x * QUARTER:(x + 1) * QUARTER] = total.astype(bf16)
+    for z in range(NZ):
+        pltpu.make_async_copy(total_v, out.at[z], sem).start()
+    pltpu.make_async_copy(out, out, sem).wait()
 
 
 def last_sum(got):
+    shape = (SLOTS, ROWS, WIDTH)
     return pl.pallas_call(
         last_sum_kernel,
         in_specs=[VMEM],
-        out_specs=VMEM,
-        out_shape=jax.ShapeDtypeStruct((NZ,) + got.shape[1:], bf16),
+        out_specs=HBM,
+        out_shape=jax.ShapeDtypeStruct((NZ,) + shape, bf16),
+        scratch_shapes=[pltpu.VMEM(shape, bf16), pltpu.SemaphoreType.DMA],
         compiler_params=params(8),
         cost_estimate=cost(got.size, MIB),
     )(got)
@@ -229,17 +231,18 @@
     pair = jnp.stack([roots, swap(roots)])
     r2 = jump(pair, 2)
     r1 = jump(pair, 1)
+    part = exchange(cut_partials(activations, cotangent), ("yl", "x"))
+    place_of = slot_blocks % COL_BLOCKS * ROW_BLOCKS + slot_blocks // COL_BLOCKS
+    part = near_sum(jnp.where(slot_blocks < BLOCKS, place_of, BLOCKS), part)
+    part, r2, r1 = after(part, r2, r1)
     r3 = jump(r2, 1)
-    part = packed_partials(slot_blocks, activations, cotangent)
-    part = near_sum(exchange(part.reshape(NEAR, NYH * SLOTS, ROWS, WIDTH), ("yl", "x")))
-    part, r1, r3 = after(part, r1, r3)
-    part = last_sum(exchange(part.reshape(NYH, SLOTS, ROWS, WIDTH), "yh"))
+    part = last_sum(exchange(part, ("yh", "yl", "x")))
+    part, r3 = after(part, r3)
     r4 = jump(r3, 1)
     g_own = exchange(part, "z")
     g_own, r4 = after(g_own, r4)
     own = jnp.stack([r1, r2, r3])
-    other = swap(own)
-    w = whole_roots(place, pair, r4, own, other)
+    w = whole_roots(place, pair, r4, own, swap(own))
     return final(place, g_own, swap(g_own), w, left_stat, right_stat)
 
 

time: 90.4 us -> 88.6 us (0.980)
  blocking collectives: 13.6 us -> 0 us
  starting transfers between devices: 49.3 us -> 58.4 us
  waiting for transfers between devices: 14.9 us -> 17.4 us
    all_to_all x1 -> x0, blocking collectives: 13.6 us -> none  [exchange(): return lax.all_to_all(value, axes, 0, 0, tiled=True)]
    all_to_all x2 -> x3, starting transfers between devices: 14.3 us -> 22 us  [exchange(): return lax.all_to_all(value, axes, 0, 0, tiled=True)]
    all_to_all x2 -> x3, waiting for transfers between devices: 0.01 us -> 2.79 us  [exchange(): return lax.all_to_all(value, axes, 0, 0, tiled=True)]
    ppermute x4, starting transfers between devices: 18.6 us -> 21.4 us  [jump(): return lax.ppermute(value, ('z', 'core'), pairs)]
    ppermute x3, starting transfers between devices: 16.4 us -> 15.1 us  [swap(): return lax.ppermute(value, 'core', [(0, 1), (1, 0)])]
  transfers between devices with their start and end apart: 9 -> 10, of which waited for: 5 -> 6; matrix products, arithmetic and copies ran while one was open for 0% -> 0% of each run, Pallas kernels for 1% -> 4%
where the time goes in v3:
time: 88.6 us; the launch traced here: 88.1 us
  starting transfers between devices  58.4 us (66%)
  waiting for transfers between devices  17.4 us (20%)
  Pallas kernels  11.1 us (13%)
    all_to_all x3, starting transfers between devices, exchange(): return lax.all_to_all(value, axes, 0, 0, tiled=True)  22 us
    ppermute x4, starting transfers between devices, jump(): return lax.ppermute(value, ('z', 'core'), pairs)  21.4 us
    ppermute x3, starting transfers between devices, swap(): return lax.ppermute(value, 'core', [(0, 1), (1, 0)])  15.1 us
    ppermute x4, waiting for transfers between devices, jump(): return lax.ppermute(value, ('z', 'core'), pairs)  12.9 us
    pallas_call x1, Pallas kernels, cut_partials(): pl.pallas_call(partial_kernel, in_specs=[HBM, HBM], out_specs=HBM, out_sh...  4.55 us
    pallas_call x1, Pallas kernels, final(): pl.pallas_call(final_kernel, in_specs=[SMEM] + [VMEM] * 5, out_specs=(VME...  3.47 us
    all_to_all x3, waiting for transfers between devices, exchange(): return lax.all_to_all(value, axes, 0, 0, tiled=True)  2.79 us
  transfers between devices with their start and end apart: 10, of which 6 were waited for; matrix products, arithmetic and copies ran while one was open for 0% of the time, Pallas kernels for 4%

profile of v3, /device:TPU:1, one launch (start us, length us, event | category | flops | bytes accessed | tf_op | source)
XLA Modules:
  0.0 88.1 jit_solution(4668545933024667931)
XLA Ops:
  0.6 4.5 %shard_map.94 = bf16[8,48,16,128]{3,2,1,0:T(8,128)(2,1)} custom-call(bf16[24,32,1024]{2,1,0:T(8,128)(2,1)} %act.1, bf16[1024,1024]{1,0:T(8,128)(2,1)} %cot.1), custom_call_target="tpu_custom_call" | custom-call | flops 1610612736 | bytes 6291456 | tf_op jit(solution)/shard_map/pallas_call | solution.py:72
  5.2 0.0 copy-start.2
  5.2 0.0 copy-start.3
  5.2 0.0 copy-start.4
  5.2 6.0 %all-to-all-start = ((bf16[8,48,16,128]{3,2,1,0:T(8,128)(2,1)}), bf16[8,48,16,128]{3,2,1,0:T(8,128)(2,1)S(1)}, u32[]{:S(2)}, u32[]{:S(2)}) async-start(bf16[8,48,16,128]{3,2,1,0:T(8,128)(2,1)} %shard_map.94), calls=%async_computation | async-start | bytes 3145728 | tf_op jit(solution)/shard_map/all_to_all | solution.py:221
  11.2 0.0 copy-done.2
  11.2 0.0 copy-done.3
  11.3 6.5 %collective-permute-start = (bf16[2,2,32,512]{3,2,1,0:T(8,128)(2,1)S(1)}, bf16[2,2,32,512]{3,2,1,0:T(8,128)(2,1)S(1)}, u32[]{:S(2)}, u32[]{:S(2)}) collective-permute-start(bf16[2,2,32,512]{3,2,1,0:T(8,128)(2,1)S(1)} %get-tuple-element.18), channel_id=1, source_target_pairs={{0,1},{1,0},{2,3},{3,2},{4,5},{5,4},{6,7},{7,6},{8,9},{9,8},{10,11... | collective-permute-start | bytes 393224 | tf_op jit(solution)/shard_map/ppermute | solution.py:209
  17.8 1.0 %collective-permute-done = bf16[2,2,32,512]{3,2,1,0:T(8,128)(2,1)S(1)} collective-permute-done((bf16[2,2,32,512]{3,2,1,0:T(8,128)(2,1)S(1)}, bf16[2,2,32,512]{3,2,1,0:T(8,128)(2,1)S(1)}, u32[]{:S(2)}, u32[]{:S(2)}) %collective-permute-start) | collective-permute-done | bytes 131104 | tf_op jit(solution)/shard_map/ppermute | solution.py:209
  18.8 7.0 %collective-permute-start.1 = (bf16[2,2,2,32,512]{4,3,2,1,0:T(8,128)(2,1)S(1)}, bf16[2,2,2,32,512]{4,3,2,1,0:T(8,128)(2,1)S(1)}, u32[]{:S(2)}, u32[]{:S(2)}) collective-permute-start(bf16[2,2,2,32,512]{4,3,2,1,0:T(8,128)(2,1)S(1)} %pad_maximum_fusion.1.here), channel_id=1, source_target_pairs={{0,4},{1,13},{2,6},{3,15},{4,8},{5,1},{6,10},{7,3},{8,12},{9,5},{1... | collective-permute-start | bytes 786440 | tf_op jit(solution)/shard_map/ppermute | solution.py:217
  25.8 2.2 %collective-permute-start.2 = (bf16[2,2,2,32,512]{4,3,2,1,0:T(8,128)(2,1)S(1)}, bf16[2,2,2,32,512]{4,3,2,1,0:T(8,128)(2,1)S(1)}, u32[]{:S(2)}, u32[]{:S(2)}) collective-permute-start(bf16[2,2,2,32,512]{4,3,2,1,0:T(8,128)(2,1)S(1)} %pad_maximum_fusion.1.here), channel_id=1, source_target_pairs={{0,2},{1,15},{2,4},{3,1},{4,6},{5,3},{6,8},{7,5},{8,10},{9,7},{10,... | collective-permute-start | bytes 786440 | tf_op jit(solution)/shard_map/ppermute | solution.py:217
  28.0 0.0 copy-done.4
  28.0 0.0 all-to-all-done.got
  28.0 1.6 %shard_map.95 = bf16[32,2,16,128]{3,2,1,0:T(8,128)(2,1)} custom-call(s32[64]{0:T(128)S(1)} %compare_select_fusion.blocks, bf16[8,48,16,128]{3,2,1,0:T(8,128)(2,1)S(1)} %all-to-all-done.got), custom_call_target="tpu_custom_call" | custom-call | flops 786432 | bytes 3145728 | tf_op jit(solution)/shard_map/pallas_call | solution.py:102
  29.6 2.3 %collective-permute-done.1 = bf16[2,2,2,32,512]{4,3,2,1,0:T(8,128)(2,1)S(1)} collective-permute-done((bf16[2,2,2,32,512]{4,3,2,1,0:T(8,128)(2,1)S(1)}, bf16[2,2,2,32,512]{4,3,2,1,0:T(8,128)(2,1)S(1)}, u32[]{:S(2)}, u32[]{:S(2)}) %collective-permute-start.1) | collective-permute-done | bytes 262176 | tf_op jit(solution)/shard_map/ppermute | solution.py:217
  31.9 3.4 %collective-permute-done.2 = bf16[2,2,2,32,512]{4,3,2,1,0:T(8,128)(2,1)S(1)} collective-permute-done((bf16[2,2,2,32,512]{4,3,2,1,0:T(8,128)(2,1)S(1)}, bf16[2,2,2,32,512]{4,3,2,1,0:T(8,128)(2,1)S(1)}, u32[]{:S(2)}, u32[]{:S(2)}) %collective-permute-start.2) | collective-permute-done | bytes 262176 | tf_op jit(solution)/shard_map/ppermute | solution.py:217
  35.3 8.7 %all-to-all-start.1 = ((bf16[32,2,16,128]{3,2,1,0:T(8,128)(2,1)}), bf16[32,2,16,128]{3,2,1,0:T(8,128)(2,1)S(1)}, u32[]{:S(2)}, u32[]{:S(2)}) async-start(bf16[32,2,16,128]{3,2,1,0:T(8,128)(2,1)} %shard_map.95), calls=%async_computation.1 | async-start | bytes 524288 | tf_op jit(solution)/shard_map/all_to_all | solution.py:221
  44.0 7.6 %collective-permute-start.3 = (bf16[2,2,2,32,512]{4,3,2,1,0:T(8,128)(2,1)S(1)}, bf16[2,2,2,32,512]{4,3,2,1,0:T(8,128)(2,1)S(1)}, u32[]{:S(2)}, u32[]{:S(2)}) collective-permute-start(bf16[2,2,2,32,512]{4,3,2,1,0:T(8,128)(2,1)S(1)} %collective-permute-done.1), channel_id=1, source_target_pairs={{0,2},{1,15},{2,4},{3,1},{4,6},{5,3},{6,8},{7,5},{8,10},{9,7},{10,... | collective-permute-start | bytes 786440 | tf_op jit(solution)/shard_map/ppermute | solution.py:217
  51.6 2.8 %all-to-all-done.1.got = bf16[32,2,16,128]{3,2,1,0:T(8,128)(2,1)S(1)} async-done(((bf16[32,2,16,128]{3,2,1,0:T(8,128)(2,1)}), bf16[32,2,16,128]{3,2,1,0:T(8,128)(2,1)S(1)}, u32[]{:S(2)}, u32[]{:S(2)}) %all-to-all-start.1) | async-done | bytes 262176 | tf_op jit(solution)/shard_map/all_to_all | solution.py:221
  54.4 0.8 shard_map.96
  55.2 0.0 collective-permute-done.3
  55.2 7.3 %all-to-all-start.2 = ((bf16[8,2,32,512]{3,2,1,0:T(8,128)(2,1)}), bf16[8,2,32,512]{3,2,1,0:T(8,128)(2,1)S(1)}, u32[]{:S(2)}, u32[]{:S(2)}) async-start(bf16[8,2,32,512]{3,2,1,0:T(8,128)(2,1)} %shard_map.96), calls=%async_computation.2 | async-start | bytes 1048576 | tf_op jit(solution)/shard_map/all_to_all | solution.py:221
  62.5 4.6 %collective-permute-start.4 = (bf16[2,2,2,32,512]{4,3,2,1,0:T(8,128)(2,1)S(1)}, bf16[2,2,2,32,512]{4,3,2,1,0:T(8,128)(2,1)S(1)}, u32[]{:S(2)}, u32[]{:S(2)}) collective-permute-start(bf16[2,2,2,32,512]{4,3,2,1,0:T(8,128)(2,1)S(1)} %collective-permute-done.3), channel_id=1, source_target_pairs={{0,2},{1,15},{2,4},{3,1},{4,6},{5,3},{6,8},{7,5},{8,10},{9,7},{10,... | collective-permute-start | bytes 786440 | tf_op jit(solution)/shard_map/ppermute | solution.py:217
  67.1 0.1 pad_maximum_fusion.own
  67.2 4.5 %collective-permute-start.6 = (bf16[3,2,2,2,32,512]{5,4,3,2,1,0:T(8,128)(2,1)S(1)}, bf16[3,2,2,2,32,512]{5,4,3,2,1,0:T(8,128)(2,1)S(1)}, u32[]{:S(2)}, u32[]{:S(2)}) collective-permute-start(bf16[3,2,2,2,32,512]{5,4,3,2,1,0:T(8,128)(2,1)S(1)} %pad_maximum_fusion.own), channel_id=1, source_target_pairs={{0,1},{1,0},{2,3},{3,2},{4,5},{5,4},{6,7},{7,6},{8,9},{9,8},{10,11... | collective-permute-start | bytes 2359304 | tf_op jit(solution)/shard_map/ppermute | solution.py:209
  71.7 7.3 %collective-permute-done.4.far = bf16[2,2,2,32,512]{4,3,2,1,0:T(8,128)(2,1)S(1)} collective-permute-done((bf16[2,2,2,32,512]{4,3,2,1,0:T(8,128)(2,1)S(1)}, bf16[2,2,2,32,512]{4,3,2,1,0:T(8,128)(2,1)S(1)}, u32[]{:S(2)}, u32[]{:S(2)}) %collective-permute-start.4) | collective-permute-done | bytes 262176 | tf_op jit(solution)/shard_map/ppermute | solution.py:217
  79.0 0.0 all-to-all-done.2.g_own
  79.0 4.1 %collective-permute-start.5 = (bf16[8,2,32,512]{3,2,1,0:T(8,128)(2,1)S(1)}, bf16[8,2,32,512]{3,2,1,0:T(8,128)(2,1)S(1)}, u32[]{:S(2)}, u32[]{:S(2)}) collective-permute-start(bf16[8,2,32,512]{3,2,1,0:T(8,128)(2,1)S(1)} %all-to-all-done.2.g_own), channel_id=1, source_target_pairs={{0,1},{1,0},{2,3},{3,2},{4,5},{5,4},{6,7},{7,6},{8,9},{9,8},{10,11... | collective-permute-start | bytes 1572872 | tf_op jit(solution)/shard_map/ppermute | solution.py:209
  83.1 0.1 pad_add_fusion.place
  83.2 0.0 copy-start
  83.2 0.0 copy-start.1
  83.2 0.0 collective-permute-done.6.other
  83.2 0.7 shard_map.97.w
  83.9 0.7 collective-permute-done.5.g_other
  84.6 0.0 copy-done
  84.6 0.0 copy-done.1
  84.6 3.5 %shard_map.98 = (f32[2,32,512]{2,1,0:T(8,128)}, f32[2,32,512]{2,1,0:T(8,128)}, bf16[2,512,512]{2,1,0:T(8,128)(2,1)}) custom-call(s32[2]{0:T(128)S(1)} %pad_add_fusion.place, bf16[8,2,32,512]{3,2,1,0:T(8,128)(2,1)S(1)} %all-to-all-done.2.g_own, bf16[8,2,32,512]{3,2,1,0:T(8,128)(2,1)S(1)} %collective-permute-done.5.g_other, ...), custom_call_target="tpu_custom_call" | custom-call | flops 1200000000 | bytes 8388608 | tf_op jit(solution)/shard_map/pallas_call | solution.py:193
  (3 shorter events, 0.1 us)
Async XLA Ops:
  5.2 6.0 %copy-start.2 = (bf16[2,32,512]{2,1,0:T(8,128)(2,1)S(1)}, bf16[2,32,512]{2,1,0:T(8,128)(2,1)}, u32[]{:S(2)}) copy-start(bf16[2,32,512]{2,1,0:T(8,128)(2,1)} %param.13) | copy-start | bytes 196612
  5.2 6.0 %copy-start.3 = (bf16[2,32,512]{2,1,0:T(8,128)(2,1)S(1)}, bf16[2,32,512]{2,1,0:T(8,128)(2,1)}, u32[]{:S(2)}) copy-start(bf16[2,32,512]{2,1,0:T(8,128)(2,1)} %param.12) | copy-start | bytes 196612
  5.2 22.8 %copy-start.4 = (s32[64]{0:T(128)S(1)}, s32[64]{0:T(128)}, u32[]{:S(2)}) copy-start(s32[64]{0:T(128)} %param.9) | copy-start | bytes 772
  5.2 22.8 %all-to-all-start = ((bf16[8,48,16,128]{3,2,1,0:T(8,128)(2,1)}), bf16[8,48,16,128]{3,2,1,0:T(8,128)(2,1)S(1)}, u32[]{:S(2)}, u32[]{:S(2)}) async-start(bf16[8,48,16,128]{3,2,1,0:T(8,128)(2,1)} %shard_map.94), calls=%async_computation | async-start | bytes 3145728 | tf_op jit(solution)/shard_map/all_to_all | solution.py:221
  11.3 7.5 %collective-permute-start = (bf16[2,2,32,512]{3,2,1,0:T(8,128)(2,1)S(1)}, bf16[2,2,32,512]{3,2,1,0:T(8,128)(2,1)S(1)}, u32[]{:S(2)}, u32[]{:S(2)}) collective-permute-start(bf16[2,2,32,512]{3,2,1,0:T(8,128)(2,1)S(1)} %get-tuple-element.18), channel_id=1, source_target_pairs={{0,1},{1,0},{2,3},{3,2},{4,5},{5,4},{6,7},{7,6},{8,9},{9,8},{10,11... | collective-permute-start | bytes 393224 | tf_op jit(solution)/shard_map/ppermute | solution.py:209
  18.8 13.1 %collective-permute-start.1 = (bf16[2,2,2,32,512]{4,3,2,1,0:T(8,128)(2,1)S(1)}, bf16[2,2,2,32,512]{4,3,2,1,0:T(8,128)(2,1)S(1)}, u32[]{:S(2)}, u32[]{:S(2)}) collective-permute-start(bf16[2,2,2,32,512]{4,3,2,1,0:T(8,128)(2,1)S(1)} %pad_maximum_fusion.1.here), channel_id=1, source_target_pairs={{0,4},{1,13},{2,6},{3,15},{4,8},{5,1},{6,10},{7,3},{8,12},{9,5},{1... | collective-permute-start | bytes 786440 | tf_op jit(solution)/shard_map/ppermute | solution.py:217
  25.8 9.5 %collective-permute-start.2 = (bf16[2,2,2,32,512]{4,3,2,1,0:T(8,128)(2,1)S(1)}, bf16[2,2,2,32,512]{4,3,2,1,0:T(8,128)(2,1)S(1)}, u32[]{:S(2)}, u32[]{:S(2)}) collective-permute-start(bf16[2,2,2,32,512]{4,3,2,1,0:T(8,128)(2,1)S(1)} %pad_maximum_fusion.1.here), channel_id=1, source_target_pairs={{0,2},{1,15},{2,4},{3,1},{4,6},{5,3},{6,8},{7,5},{8,10},{9,7},{10,... | collective-permute-start | bytes 786440 | tf_op jit(solution)/shard_map/ppermute | solution.py:217
  35.3 19.1 %all-to-all-start.1 = ((bf16[32,2,16,128]{3,2,1,0:T(8,128)(2,1)}), bf16[32,2,16,128]{3,2,1,0:T(8,128)(2,1)S(1)}, u32[]{:S(2)}, u32[]{:S(2)}) async-start(bf16[32,2,16,128]{3,2,1,0:T(8,128)(2,1)} %shard_map.95), calls=%async_computation.1 | async-start | bytes 524288 | tf_op jit(solution)/shard_map/all_to_all | solution.py:221
  44.0 11.2 %collective-permute-start.3 = (bf16[2,2,2,32,512]{4,3,2,1,0:T(8,128)(2,1)S(1)}, bf16[2,2,2,32,512]{4,3,2,1,0:T(8,128)(2,1)S(1)}, u32[]{:S(2)}, u32[]{:S(2)}) collective-permute-start(bf16[2,2,2,32,512]{4,3,2,1,0:T(8,128)(2,1)S(1)} %collective-permute-done.1), channel_id=1, source_target_pairs={{0,2},{1,15},{2,4},{3,1},{4,6},{5,3},{6,8},{7,5},{8,10},{9,7},{10,... | collective-permute-start | bytes 786440 | tf_op jit(solution)/shard_map/ppermute | solution.py:217
  55.2 23.8 %all-to-all-start.2 = ((bf16[8,2,32,512]{3,2,1,0:T(8,128)(2,1)}), bf16[8,2,32,512]{3,2,1,0:T(8,128)(2,1)S(1)}, u32[]{:S(2)}, u32[]{:S(2)}) async-start(bf16[8,2,32,512]{3,2,1,0:T(8,128)(2,1)} %shard_map.96), calls=%async_computation.2 | async-start | bytes 1048576 | tf_op jit(solution)/shard_map/all_to_all | solution.py:221
  62.5 16.5 %collective-permute-start.4 = (bf16[2,2,2,32,512]{4,3,2,1,0:T(8,128)(2,1)S(1)}, bf16[2,2,2,32,512]{4,3,2,1,0:T(8,128)(2,1)S(1)}, u32[]{:S(2)}, u32[]{:S(2)}) collective-permute-start(bf16[2,2,2,32,512]{4,3,2,1,0:T(8,128)(2,1)S(1)} %collective-permute-done.3), channel_id=1, source_target_pairs={{0,2},{1,15},{2,4},{3,1},{4,6},{5,3},{6,8},{7,5},{8,10},{9,7},{10,... | collective-permute-start | bytes 786440 | tf_op jit(solution)/shard_map/ppermute | solution.py:217
  67.2 16.0 %collective-permute-start.6 = (bf16[3,2,2,2,32,512]{5,4,3,2,1,0:T(8,128)(2,1)S(1)}, bf16[3,2,2,2,32,512]{5,4,3,2,1,0:T(8,128)(2,1)S(1)}, u32[]{:S(2)}, u32[]{:S(2)}) collective-permute-start(bf16[3,2,2,2,32,512]{5,4,3,2,1,0:T(8,128)(2,1)S(1)} %pad_maximum_fusion.own), channel_id=1, source_target_pairs={{0,1},{1,0},{2,3},{3,2},{4,5},{5,4},{6,7},{7,6},{8,9},{9,8},{10,11... | collective-permute-start | bytes 2359304 | tf_op jit(solution)/shard_map/ppermute | solution.py:209
  79.0 5.6 %collective-permute-start.5 = (bf16[8,2,32,512]{3,2,1,0:T(8,128)(2,1)S(1)}, bf16[8,2,32,512]{3,2,1,0:T(8,128)(2,1)S(1)}, u32[]{:S(2)}, u32[]{:S(2)}) collective-permute-start(bf16[8,2,32,512]{3,2,1,0:T(8,128)(2,1)S(1)} %all-to-all-done.2.g_own), channel_id=1, source_target_pairs={{0,1},{1,0},{2,3},{3,2},{4,5},{5,4},{6,7},{7,6},{8,9},{9,8},{10,11... | collective-permute-start | bytes 1572872 | tf_op jit(solution)/shard_map/ppermute | solution.py:209
  83.2 1.4 %copy-start = (f32[2,32,512]{2,1,0:T(8,128)S(1)}, f32[2,32,512]{2,1,0:T(8,128)}, u32[]{:S(2)}) copy-start(f32[2,32,512]{2,1,0:T(8,128)} %left_stat.1) | copy-start | bytes 393220
  83.2 1.4 %copy-start.1 = (f32[2,32,512]{2,1,0:T(8,128)S(1)}, f32[2,32,512]{2,1,0:T(8,128)}, u32[]{:S(2)}) copy-start(f32[2,32,512]{2,1,0:T(8,128)} %right_stat.1) | copy-start | bytes 393220

commit v4 on v3

--- a/solution.py
+++ b/solution.py
@@ -5,12 +5,13 @@
 from jax.experimental.pallas import tpu as pltpu
 from jax.sharding import Mesh, PartitionSpec as P
 
-NYH, NYL, NX, NZ, NC = 4, 2, 4, 8, 2
-NEAR = NYL * NX
+NY, NX, NZ, NC = 8, 4, 8, 2
+PAIR = 2
+NEAR = PAIR * PAIR
 ROW_BLOCKS, COL_BLOCKS, SLOTS = 24, 2, 2
 BLOCKS = ROW_BLOCKS * COL_BLOCKS
 ROWS, WIDTH = 32, 512
-HALF, QUARTER = ROWS // NYL, WIDTH // NX
+HALF, SIDE = ROWS // PAIR, WIDTH // PAIR
 PARTS = 2
 DECAY = 0.95
 bf16, f32 = jnp.bfloat16, jnp.float32
@@ -58,17 +59,17 @@
             part = jnp.dot(a, cot_v[:, j * WIDTH:(j + 1) * WIDTH], preferred_element_type=f32)
             part = part.astype(bf16).reshape(per, ROWS, WIDTH)
             span = slice(j * ROW_BLOCKS + p * per, j * ROW_BLOCKS + (p + 1) * per)
-            for yl in range(NYL):
-                for x in range(NX):
-                    piece = part[:, yl * HALF:(yl + 1) * HALF, x * QUARTER:(x + 1) * QUARTER]
-                    cut[yl * NX + x, span] = piece
+            for top in range(PAIR):
+                for left in range(PAIR):
+                    piece = part[:, top * HALF:(top + 1) * HALF, left * SIDE:(left + 1) * SIDE]
+                    cut[top * PAIR + left, span] = piece
         out_copy(j).start()
     for j in range(COL_BLOCKS):
         out_copy(j).wait()
 
 
 def cut_partials(activations, cotangent):
-    shape = (NEAR, BLOCKS, HALF, QUARTER)
+    shape = (NEAR, BLOCKS, HALF, SIDE)
     return pl.pallas_call(
         partial_kernel,
         in_specs=[HBM, HBM],
@@ -92,8 +93,8 @@
     for n in range(1, NEAR):
         total += got[n].astype(f32)
     total_v[:BLOCKS] = total.astype(bf16)
-    total_v[BLOCKS] = jnp.zeros((HALF, QUARTER), bf16)
-    for owner in range(NYH * NEAR):
+    total_v[BLOCKS] = jnp.zeros((HALF, SIDE), bf16)
+    for owner in range(NY * NX):
         for t in range(SLOTS):
             out[owner, t] = total_v[blocks[owner * SLOTS + t]]
 
@@ -103,36 +104,40 @@
         near_sum_kernel,
         in_specs=[SMEM, VMEM],
         out_specs=VMEM,
-        out_shape=jax.ShapeDtypeStruct((NYH * NEAR, SLOTS, HALF, QUARTER), bf16),
-        scratch_shapes=[pltpu.VMEM((BLOCKS + 1, HALF, QUARTER), bf16)],
+        out_shape=jax.ShapeDtypeStruct((NY * NX, SLOTS, HALF, SIDE), bf16),
+        scratch_shapes=[pltpu.VMEM((BLOCKS + 1, HALF, SIDE), bf16)],
         compiler_params=params(16),
         cost_estimate=cost(got.size, 3 * MIB),
     )(blocks, got)
 
 
-def last_sum_kernel(got, out, total_v, sem):
-    for yl in range(NYL):
-        for x in range(NX):
-            total = got[yl * NX + x].astype(f32)
-            for yh in range(1, NYH):
-                total += got[yh * NEAR + yl * NX + x].astype(f32)
-            total_v[:, yl * HALF:(yl + 1) * HALF, x * QUARTER:(x + 1) * QUARTER] = total.astype(bf16)
+def last_sum_kernel(place, got, out, total_v, sem):
+    core = place[0]
+    for odd_y in range(PAIR):
+        for odd_x in range(PAIR):
+            total = jnp.zeros(got.shape[1:], f32)
+            for y in range(odd_y, NY, PAIR):
+                for x in range(odd_x, NX, PAIR):
+                    total += got[y * NX + x].astype(f32)
+            row = pl.ds(pl.multiple_of(lax.rem(odd_y + core, PAIR) * HALF, HALF), HALF)
+            col = pl.ds(pl.multiple_of(lax.rem(odd_x + core, PAIR) * SIDE, SIDE), SIDE)
+            total_v[:, row, col] = total.astype(bf16)
     for z in range(NZ):
         pltpu.make_async_copy(total_v, out.at[z], sem).start()
     pltpu.make_async_copy(out, out, sem).wait()
 
 
-def last_sum(got):
+def last_sum(place, got):
     shape = (SLOTS, ROWS, WIDTH)
     return pl.pallas_call(
         last_sum_kernel,
-        in_specs=[VMEM],
+        in_specs=[SMEM, VMEM],
         out_specs=HBM,
         out_shape=jax.ShapeDtypeStruct((NZ,) + shape, bf16),
         scratch_shapes=[pltpu.VMEM(shape, bf16), pltpu.SemaphoreType.DMA],
         compiler_params=params(8),
         cost_estimate=cost(got.size, MIB),
-    )(got)
+    )(place, got)
 
 
 def rows_of(z, core):
@@ -217,8 +222,18 @@
     return lax.ppermute(value, ("z", "core"), pairs)
 
 
-def exchange(value, axes):
-    return lax.all_to_all(value, axes, 0, 0, tiled=True)
+def exchange(value, axes, groups=None):
+    return lax.all_to_all(value, axes, 0, 0, axis_index_groups=groups, tiled=True)
+
+
+def squares():
+    groups = []
+    for core in range(NC):
+        for y in range(0, NY, PAIR):
+            for x in range(0, NX, PAIR):
+                members = [((y + core + a) % NY, (x + core + b) % NX) for a in range(PAIR) for b in range(PAIR)]
+                groups.append([(my * NX + mx) * NC + core for my, mx in members])
+    return groups
 
 
 def after(value, *others):
@@ -229,15 +244,15 @@
     place = jnp.stack([lax.axis_index("core"), lax.axis_index("z")]).astype(jnp.int32)
     roots = jnp.stack([left_root, right_root])
     pair = jnp.stack([roots, swap(roots)])
-    r2 = jump(pair, 2)
     r1 = jump(pair, 1)
-    part = exchange(cut_partials(activations, cotangent), ("yl", "x"))
+    part = exchange(cut_partials(activations, cotangent), ("y", "x", "core"), squares())
     place_of = slot_blocks % COL_BLOCKS * ROW_BLOCKS + slot_blocks // COL_BLOCKS
     part = near_sum(jnp.where(slot_blocks < BLOCKS, place_of, BLOCKS), part)
-    part, r2, r1 = after(part, r2, r1)
+    part, r1 = after(part, r1)
+    r2 = jump(r1, 1)
     r3 = jump(r2, 1)
-    part = last_sum(exchange(part, ("yh", "yl", "x")))
-    part, r3 = after(part, r3)
+    part = last_sum(place, exchange(part, ("y", "x")))
+    part, r2, r3 = after(part, r2, r3)
     r4 = jump(r3, 1)
     g_own = exchange(part, "z")
     g_own, r4 = after(g_own, r4)
@@ -247,8 +262,8 @@
 
 
 def solution(mesh):
-    grid = Mesh(mesh.devices.reshape(NYH, NYL, NX, NZ, NC), ("yh", "yl", "x", "z", "core"))
-    dp, mp = ("yh", "yl", "x"), ("z", "core")
+    grid = Mesh(mesh.devices.reshape(NY, NX, NZ, NC), ("y", "x", "z", "core"))
+    dp, mp = ("y", "x"), ("z", "core")
     return jax.shard_map(
         local,
         mesh=grid,

time: 88.6 us -> 87.6 us (0.989)
  waiting for transfers between devices: 17.4 us -> 16.1 us
    ppermute x4, starting transfers between devices: 21.4 us -> 26.1 us  [jump(): return lax.ppermute(value, ('z', 'core'), pairs)]
    ppermute x3, starting transfers between devices: 15.1 us -> 10.8 us  [swap(): return lax.ppermute(value, 'core', [(0, 1), (1, 0)])]
    all_to_all x3, waiting for transfers between devices: 2.79 us -> 0.6 us  [exchange(): lax.all_to_all(value, axes, 0, 0, axis_index_groups=groups, tiled=True)]
    all_to_all x3, starting transfers between devices: 22 us -> 21.1 us  [exchange(): lax.all_to_all(value, axes, 0, 0, axis_index_groups=groups, tiled=True)]
  transfers between devices with their start and end apart: 10 -> 10, of which waited for: 6 -> 7; matrix products, arithmetic and copies ran while one was open for 0% -> 0% of each run, Pallas kernels for 4% -> 4%
where the time goes in v4:
time: 87.6 us; the launch traced here: 87 us
  starting transfers between devices  58 us (66%)
  waiting for transfers between devices  16.1 us (18%)
  Pallas kernels  11.8 us (13%)
    ppermute x4, starting transfers between devices, jump(): return lax.ppermute(value, ('z', 'core'), pairs)  26.1 us
    all_to_all x3, starting transfers between devices, exchange(): lax.all_to_all(value, axes, 0, 0, axis_index_groups=groups, tiled=True)  21.1 us
    ppermute x4, waiting for transfers between devices, jump(): return lax.ppermute(value, ('z', 'core'), pairs)  13.7 us
    ppermute x3, starting transfers between devices, swap(): return lax.ppermute(value, 'core', [(0, 1), (1, 0)])  10.8 us
    pallas_call x1, Pallas kernels, cut_partials(): pl.pallas_call(partial_kernel, in_specs=[HBM, HBM], out_specs=HBM, out_sh...  4.55 us
    pallas_call x1, Pallas kernels, final(): pl.pallas_call(final_kernel, in_specs=[SMEM] + [VMEM] * 5, out_specs=(VME...  3.47 us
    ppermute x3, waiting for transfers between devices, swap(): return lax.ppermute(value, 'core', [(0, 1), (1, 0)])  1.78 us
  transfers between devices with their start and end apart: 10, of which 7 were waited for; matrix products, arithmetic and copies ran while one was open for 0% of the time, Pallas kernels for 4%

profile of v4, /device:TPU:1, one launch (start us, length us, event | category | flops | bytes accessed | tf_op | source)
XLA Modules:
  0.0 87.0 jit_solution(16660067612366662963)
XLA Ops:
  0.6 4.6 %shard_map.94 = bf16[4,48,16,256]{3,2,1,0:T(8,128)(2,1)} custom-call(bf16[24,32,1024]{2,1,0:T(8,128)(2,1)} %act.1, bf16[1024,1024]{1,0:T(8,128)(2,1)} %cot.1), custom_call_target="tpu_custom_call" | custom-call | flops 1610612736 | bytes 6291456 | tf_op jit(solution)/shard_map/pallas_call | solution.py:73
  5.2 0.0 copy-start.2
  5.2 0.0 copy-start.3
  5.2 0.0 copy-start.4
  5.2 9.9 %all-to-all-start = ((bf16[4,48,16,256]{3,2,1,0:T(8,128)(2,1)}), bf16[4,48,16,256]{3,2,1,0:T(8,128)(2,1)S(1)}, u32[]{:S(2)}, u32[]{:S(2)}) async-start(bf16[4,48,16,256]{3,2,1,0:T(8,128)(2,1)} %shard_map.94), calls=%async_computation | async-start | bytes 3145728 | tf_op jit(solution)/shard_map/all_to_all | solution.py:226
  15.1 0.0 copy-done.2
  15.1 0.0 copy-done.3
  15.1 2.6 %collective-permute-start = (bf16[2,2,32,512]{3,2,1,0:T(8,128)(2,1)S(1)}, bf16[2,2,32,512]{3,2,1,0:T(8,128)(2,1)S(1)}, u32[]{:S(2)}, u32[]{:S(2)}) collective-permute-start(bf16[2,2,32,512]{3,2,1,0:T(8,128)(2,1)S(1)} %get-tuple-element.18), channel_id=1, source_target_pairs={{0,1},{1,0},{2,3},{3,2},{4,5},{5,4},{6,7},{7,6},{8,9},{9,8},{10,11... | collective-permute-start | bytes 393224 | tf_op jit(solution)/shard_map/ppermute | solution.py:214
  17.8 1.0 %collective-permute-done = bf16[2,2,32,512]{3,2,1,0:T(8,128)(2,1)S(1)} collective-permute-done((bf16[2,2,32,512]{3,2,1,0:T(8,128)(2,1)S(1)}, bf16[2,2,32,512]{3,2,1,0:T(8,128)(2,1)S(1)}, u32[]{:S(2)}, u32[]{:S(2)}) %collective-permute-start) | collective-permute-done | bytes 131104 | tf_op jit(solution)/shard_map/ppermute | solution.py:214
  18.8 10.3 %collective-permute-start.1 = (bf16[2,2,2,32,512]{4,3,2,1,0:T(8,128)(2,1)S(1)}, bf16[2,2,2,32,512]{4,3,2,1,0:T(8,128)(2,1)S(1)}, u32[]{:S(2)}, u32[]{:S(2)}) collective-permute-start(bf16[2,2,2,32,512]{4,3,2,1,0:T(8,128)(2,1)S(1)} %pad_maximum_fusion.1.here), channel_id=1, source_target_pairs={{0,2},{1,15},{2,4},{3,1},{4,6},{5,3},{6,8},{7,5},{8,10},{9,7},{10,... | collective-permute-start | bytes 786440 | tf_op jit(solution)/shard_map/ppermute | solution.py:222
  29.1 0.0 copy-done.4
  29.1 0.0 all-to-all-done.got
  29.1 1.7 %shard_map.95 = bf16[32,2,16,256]{3,2,1,0:T(8,128)(2,1)} custom-call(s32[64]{0:T(128)S(1)} %compare_select_fusion.blocks, bf16[4,48,16,256]{3,2,1,0:T(8,128)(2,1)S(1)} %all-to-all-done.got), custom_call_target="tpu_custom_call" | custom-call | flops 786432 | bytes 3145728 | tf_op jit(solution)/shard_map/pallas_call | solution.py:103
  30.9 1.5 %collective-permute-done.1 = bf16[2,2,2,32,512]{4,3,2,1,0:T(8,128)(2,1)S(1)} collective-permute-done((bf16[2,2,2,32,512]{4,3,2,1,0:T(8,128)(2,1)S(1)}, bf16[2,2,2,32,512]{4,3,2,1,0:T(8,128)(2,1)S(1)}, u32[]{:S(2)}, u32[]{:S(2)}) %collective-permute-start.1) | collective-permute-done | bytes 262176 | tf_op jit(solution)/shard_map/ppermute | solution.py:222
  32.4 5.6 %all-to-all-start.1 = ((bf16[32,2,16,256]{3,2,1,0:T(8,128)(2,1)}), bf16[32,2,16,256]{3,2,1,0:T(8,128)(2,1)S(1)}, u32[]{:S(2)}, u32[]{:S(2)}) async-start(bf16[32,2,16,256]{3,2,1,0:T(8,128)(2,1)} %shard_map.95), calls=%async_computation.1 | async-start | bytes 1048576 | tf_op jit(solution)/shard_map/all_to_all | solution.py:226
  38.0 6.0 %collective-permute-start.2 = (bf16[2,2,2,32,512]{4,3,2,1,0:T(8,128)(2,1)S(1)}, bf16[2,2,2,32,512]{4,3,2,1,0:T(8,128)(2,1)S(1)}, u32[]{:S(2)}, u32[]{:S(2)}) collective-permute-start(bf16[2,2,2,32,512]{4,3,2,1,0:T(8,128)(2,1)S(1)} %collective-permute-done.1), channel_id=1, source_target_pairs={{0,2},{1,15},{2,4},{3,1},{4,6},{5,3},{6,8},{7,5},{8,10},{9,7},{10,... | collective-permute-start | bytes 786440 | tf_op jit(solution)/shard_map/ppermute | solution.py:222
  44.0 3.3 %collective-permute-done.2 = bf16[2,2,2,32,512]{4,3,2,1,0:T(8,128)(2,1)S(1)} collective-permute-done((bf16[2,2,2,32,512]{4,3,2,1,0:T(8,128)(2,1)S(1)}, bf16[2,2,2,32,512]{4,3,2,1,0:T(8,128)(2,1)S(1)}, u32[]{:S(2)}, u32[]{:S(2)}) %collective-permute-start.2) | collective-permute-done | bytes 262176 | tf_op jit(solution)/shard_map/ppermute | solution.py:222
  47.2 5.3 %collective-permute-start.3 = (bf16[2,2,2,32,512]{4,3,2,1,0:T(8,128)(2,1)S(1)}, bf16[2,2,2,32,512]{4,3,2,1,0:T(8,128)(2,1)S(1)}, u32[]{:S(2)}, u32[]{:S(2)}) collective-permute-start(bf16[2,2,2,32,512]{4,3,2,1,0:T(8,128)(2,1)S(1)} %collective-permute-done.2), channel_id=1, source_target_pairs={{0,2},{1,15},{2,4},{3,1},{4,6},{5,3},{6,8},{7,5},{8,10},{9,7},{10,... | collective-permute-start | bytes 786440 | tf_op jit(solution)/shard_map/ppermute | solution.py:222
  52.6 0.1 pad_add_fusion.place
  52.6 0.6 all-to-all-done.1.got
  53.2 1.4 %shard_map.96 = bf16[8,2,32,512]{3,2,1,0:T(8,128)(2,1)} custom-call(s32[2]{0:T(128)S(1)} %pad_add_fusion.place, bf16[32,2,16,256]{3,2,1,0:T(8,128)(2,1)S(1)} %all-to-all-done.1.got), custom_call_target="tpu_custom_call" | custom-call | flops 262144 | bytes 1048576 | tf_op jit(solution)/shard_map/pallas_call | solution.py:132
  54.6 1.2 %collective-permute-done.3 = bf16[2,2,2,32,512]{4,3,2,1,0:T(8,128)(2,1)S(1)} collective-permute-done((bf16[2,2,2,32,512]{4,3,2,1,0:T(8,128)(2,1)S(1)}, bf16[2,2,2,32,512]{4,3,2,1,0:T(8,128)(2,1)S(1)}, u32[]{:S(2)}, u32[]{:S(2)}) %collective-permute-start.3) | collective-permute-done | bytes 262176 | tf_op jit(solution)/shard_map/ppermute | solution.py:222
  55.9 5.6 %all-to-all-start.2 = ((bf16[8,2,32,512]{3,2,1,0:T(8,128)(2,1)}), bf16[8,2,32,512]{3,2,1,0:T(8,128)(2,1)S(1)}, u32[]{:S(2)}, u32[]{:S(2)}) async-start(bf16[8,2,32,512]{3,2,1,0:T(8,128)(2,1)} %shard_map.96), calls=%async_computation.2 | async-start | bytes 1048576 | tf_op jit(solution)/shard_map/all_to_all | solution.py:226
  61.4 4.6 %collective-permute-start.4 = (bf16[2,2,2,32,512]{4,3,2,1,0:T(8,128)(2,1)S(1)}, bf16[2,2,2,32,512]{4,3,2,1,0:T(8,128)(2,1)S(1)}, u32[]{:S(2)}, u32[]{:S(2)}) collective-permute-start(bf16[2,2,2,32,512]{4,3,2,1,0:T(8,128)(2,1)S(1)} %collective-permute-done.3), channel_id=1, source_target_pairs={{0,2},{1,15},{2,4},{3,1},{4,6},{5,3},{6,8},{7,5},{8,10},{9,7},{10,... | collective-permute-start | bytes 786440 | tf_op jit(solution)/shard_map/ppermute | solution.py:222
  66.0 0.1 pad_maximum_fusion.own
  66.1 0.0 copy-start
  66.1 0.0 copy-start.1
  66.1 4.0 %collective-permute-start.6 = (bf16[3,2,2,2,32,512]{5,4,3,2,1,0:T(8,128)(2,1)S(1)}, bf16[3,2,2,2,32,512]{5,4,3,2,1,0:T(8,128)(2,1)S(1)}, u32[]{:S(2)}, u32[]{:S(2)}) collective-permute-start(bf16[3,2,2,2,32,512]{5,4,3,2,1,0:T(8,128)(2,1)S(1)} %pad_maximum_fusion.own), channel_id=1, source_target_pairs={{0,1},{1,0},{2,3},{3,2},{4,5},{5,4},{6,7},{7,6},{8,9},{9,8},{10,11... | collective-permute-start | bytes 2359304 | tf_op jit(solution)/shard_map/ppermute | solution.py:214
  70.1 7.7 %collective-permute-done.4.far = bf16[2,2,2,32,512]{4,3,2,1,0:T(8,128)(2,1)S(1)} collective-permute-done((bf16[2,2,2,32,512]{4,3,2,1,0:T(8,128)(2,1)S(1)}, bf16[2,2,2,32,512]{4,3,2,1,0:T(8,128)(2,1)S(1)}, u32[]{:S(2)}, u32[]{:S(2)}) %collective-permute-start.4) | collective-permute-done | bytes 262176 | tf_op jit(solution)/shard_map/ppermute | solution.py:222
  77.8 0.0 all-to-all-done.2.g_own
  77.8 4.2 %collective-permute-start.5 = (bf16[8,2,32,512]{3,2,1,0:T(8,128)(2,1)S(1)}, bf16[8,2,32,512]{3,2,1,0:T(8,128)(2,1)S(1)}, u32[]{:S(2)}, u32[]{:S(2)}) collective-permute-start(bf16[8,2,32,512]{3,2,1,0:T(8,128)(2,1)S(1)} %all-to-all-done.2.g_own), channel_id=1, source_target_pairs={{0,1},{1,0},{2,3},{3,2},{4,5},{5,4},{6,7},{7,6},{8,9},{9,8},{10,11... | collective-permute-start | bytes 1572872 | tf_op jit(solution)/shard_map/ppermute | solution.py:214
  82.0 0.0 collective-permute-done.6.other
  82.0 0.7 shard_map.97.w
  82.7 0.8 collective-permute-done.5.g_other
  83.5 0.0 copy-done
  83.5 0.0 copy-done.1
  83.5 3.5 %shard_map.98 = (f32[2,32,512]{2,1,0:T(8,128)}, f32[2,32,512]{2,1,0:T(8,128)}, bf16[2,512,512]{2,1,0:T(8,128)(2,1)}) custom-call(s32[2]{0:T(128)S(1)} %pad_add_fusion.place, bf16[8,2,32,512]{3,2,1,0:T(8,128)(2,1)S(1)} %all-to-all-done.2.g_own, bf16[8,2,32,512]{3,2,1,0:T(8,128)(2,1)S(1)} %collective-permute-done.5.g_other, ...), custom_call_target="tpu_custom_call" | custom-call | flops 1200000000 | bytes 8388608 | tf_op jit(solution)/shard_map/pallas_call | solution.py:198
  (3 shorter events, 0.1 us)
Async XLA Ops:
  5.2 9.9 %copy-start.2 = (bf16[2,32,512]{2,1,0:T(8,128)(2,1)S(1)}, bf16[2,32,512]{2,1,0:T(8,128)(2,1)}, u32[]{:S(2)}) copy-start(bf16[2,32,512]{2,1,0:T(8,128)(2,1)} %param.13) | copy-start | bytes 196612
  5.2 9.9 %copy-start.3 = (bf16[2,32,512]{2,1,0:T(8,128)(2,1)S(1)}, bf16[2,32,512]{2,1,0:T(8,128)(2,1)}, u32[]{:S(2)}) copy-start(bf16[2,32,512]{2,1,0:T(8,128)(2,1)} %param.12) | copy-start | bytes 196612
  5.2 23.9 %copy-start.4 = (s32[64]{0:T(128)S(1)}, s32[64]{0:T(128)}, u32[]{:S(2)}) copy-start(s32[64]{0:T(128)} %param.9) | copy-start | bytes 772
  5.2 23.9 %all-to-all-start = ((bf16[4,48,16,256]{3,2,1,0:T(8,128)(2,1)}), bf16[4,48,16,256]{3,2,1,0:T(8,128)(2,1)S(1)}, u32[]{:S(2)}, u32[]{:S(2)}) async-start(bf16[4,48,16,256]{3,2,1,0:T(8,128)(2,1)} %shard_map.94), calls=%async_computation | async-start | bytes 3145728 | tf_op jit(solution)/shard_map/all_to_all | solution.py:226
  15.1 3.6 %collective-permute-start = (bf16[2,2,32,512]{3,2,1,0:T(8,128)(2,1)S(1)}, bf16[2,2,32,512]{3,2,1,0:T(8,128)(2,1)S(1)}, u32[]{:S(2)}, u32[]{:S(2)}) collective-permute-start(bf16[2,2,32,512]{3,2,1,0:T(8,128)(2,1)S(1)} %get-tuple-element.18), channel_id=1, source_target_pairs={{0,1},{1,0},{2,3},{3,2},{4,5},{5,4},{6,7},{7,6},{8,9},{9,8},{10,11... | collective-permute-start | bytes 393224 | tf_op jit(solution)/shard_map/ppermute | solution.py:214
  18.8 13.6 %collective-permute-start.1 = (bf16[2,2,2,32,512]{4,3,2,1,0:T(8,128)(2,1)S(1)}, bf16[2,2,2,32,512]{4,3,2,1,0:T(8,128)(2,1)S(1)}, u32[]{:S(2)}, u32[]{:S(2)}) collective-permute-start(bf16[2,2,2,32,512]{4,3,2,1,0:T(8,128)(2,1)S(1)} %pad_maximum_fusion.1.here), channel_id=1, source_target_pairs={{0,2},{1,15},{2,4},{3,1},{4,6},{5,3},{6,8},{7,5},{8,10},{9,7},{10,... | collective-permute-start | bytes 786440 | tf_op jit(solution)/shard_map/ppermute | solution.py:222
  32.4 20.8 %all-to-all-start.1 = ((bf16[32,2,16,256]{3,2,1,0:T(8,128)(2,1)}), bf16[32,2,16,256]{3,2,1,0:T(8,128)(2,1)S(1)}, u32[]{:S(2)}, u32[]{:S(2)}) async-start(bf16[32,2,16,256]{3,2,1,0:T(8,128)(2,1)} %shard_map.95), calls=%async_computation.1 | async-start | bytes 1048576 | tf_op jit(solution)/shard_map/all_to_all | solution.py:226
  38.0 9.3 %collective-permute-start.2 = (bf16[2,2,2,32,512]{4,3,2,1,0:T(8,128)(2,1)S(1)}, bf16[2,2,2,32,512]{4,3,2,1,0:T(8,128)(2,1)S(1)}, u32[]{:S(2)}, u32[]{:S(2)}) collective-permute-start(bf16[2,2,2,32,512]{4,3,2,1,0:T(8,128)(2,1)S(1)} %collective-permute-done.1), channel_id=1, source_target_pairs={{0,2},{1,15},{2,4},{3,1},{4,6},{5,3},{6,8},{7,5},{8,10},{9,7},{10,... | collective-permute-start | bytes 786440 | tf_op jit(solution)/shard_map/ppermute | solution.py:222
  47.2 8.6 %collective-permute-start.3 = (bf16[2,2,2,32,512]{4,3,2,1,0:T(8,128)(2,1)S(1)}, bf16[2,2,2,32,512]{4,3,2,1,0:T(8,128)(2,1)S(1)}, u32[]{:S(2)}, u32[]{:S(2)}) collective-permute-start(bf16[2,2,2,32,512]{4,3,2,1,0:T(8,128)(2,1)S(1)} %collective-permute-done.2), channel_id=1, source_target_pairs={{0,2},{1,15},{2,4},{3,1},{4,6},{5,3},{6,8},{7,5},{8,10},{9,7},{10,... | collective-permute-start | bytes 786440 | tf_op jit(solution)/shard_map/ppermute | solution.py:222
  55.9 22.0 %all-to-all-start.2 = ((bf16[8,2,32,512]{3,2,1,0:T(8,128)(2,1)}), bf16[8,2,32,512]{3,2,1,0:T(8,128)(2,1)S(1)}, u32[]{:S(2)}, u32[]{:S(2)}) async-start(bf16[8,2,32,512]{3,2,1,0:T(8,128)(2,1)} %shard_map.96), calls=%async_computation.2 | async-start | bytes 1048576 | tf_op jit(solution)/shard_map/all_to_all | solution.py:226
  61.4 16.4 %collective-permute-start.4 = (bf16[2,2,2,32,512]{4,3,2,1,0:T(8,128)(2,1)S(1)}, bf16[2,2,2,32,512]{4,3,2,1,0:T(8,128)(2,1)S(1)}, u32[]{:S(2)}, u32[]{:S(2)}) collective-permute-start(bf16[2,2,2,32,512]{4,3,2,1,0:T(8,128)(2,1)S(1)} %collective-permute-done.3), channel_id=1, source_target_pairs={{0,2},{1,15},{2,4},{3,1},{4,6},{5,3},{6,8},{7,5},{8,10},{9,7},{10,... | collective-permute-start | bytes 786440 | tf_op jit(solution)/shard_map/ppermute | solution.py:222
  66.1 17.4 %copy-start = (f32[2,32,512]{2,1,0:T(8,128)S(1)}, f32[2,32,512]{2,1,0:T(8,128)}, u32[]{:S(2)}) copy-start(f32[2,32,512]{2,1,0:T(8,128)} %left_stat.1) | copy-start | bytes 393220
  66.1 17.4 %copy-start.1 = (f32[2,32,512]{2,1,0:T(8,128)S(1)}, f32[2,32,512]{2,1,0:T(8,128)}, u32[]{:S(2)}) copy-start(f32[2,32,512]{2,1,0:T(8,128)} %right_stat.1) | copy-start | bytes 393220
  66.1 15.9 %collective-permute-start.6 = (bf16[3,2,2,2,32,512]{5,4,3,2,1,0:T(8,128)(2,1)S(1)}, bf16[3,2,2,2,32,512]{5,4,3,2,1,0:T(8,128)(2,1)S(1)}, u32[]{:S(2)}, u32[]{:S(2)}) collective-permute-start(bf16[3,2,2,2,32,512]{5,4,3,2,1,0:T(8,128)(2,1)S(1)} %pad_maximum_fusion.own), channel_id=1, source_target_pairs={{0,1},{1,0},{2,3},{3,2},{4,5},{5,4},{6,7},{7,6},{8,9},{9,8},{10,11... | collective-permute-start | bytes 2359304 | tf_op jit(solution)/shard_map/ppermute | solution.py:214
  77.8 5.7 %collective-permute-start.5 = (bf16[8,2,32,512]{3,2,1,0:T(8,128)(2,1)S(1)}, bf16[8,2,32,512]{3,2,1,0:T(8,128)(2,1)S(1)}, u32[]{:S(2)}, u32[]{:S(2)}) collective-permute-start(bf16[8,2,32,512]{3,2,1,0:T(8,128)(2,1)S(1)} %all-to-all-done.2.g_own), channel_id=1, source_target_pairs={{0,1},{1,0},{2,3},{3,2},{4,5},{5,4},{6,7},{7,6},{8,9},{9,8},{10,11... | collective-permute-start | bytes 1572872 | tf_op jit(solution)/shard_map/ppermute | solution.py:214

commit v5 on v4

--- a/solution.py
+++ b/solution.py
@@ -88,24 +88,33 @@
     )(activations, cotangent)
 
 
-def near_sum_kernel(blocks, got, out, total_v):
+def near_sum_kernel(blocks, got, out, total_v, slots_v, sem):
     total = got[0].astype(f32)
     for n in range(1, NEAR):
         total += got[n].astype(f32)
     total_v[:BLOCKS] = total.astype(bf16)
     total_v[BLOCKS] = jnp.zeros((HALF, SIDE), bf16)
-    for owner in range(NY * NX):
-        for t in range(SLOTS):
-            out[owner, t] = total_v[blocks[owner * SLOTS + t]]
+    for y in range(NY):
+        span = pl.ds(y * NX, NX)
+        for owner in range(y * NX, (y + 1) * NX):
+            for t in range(SLOTS):
+                slots_v[owner, t] = total_v[blocks[owner * SLOTS + t]]
+        pltpu.make_async_copy(slots_v.at[span], out.at[span], sem).start()
+    pltpu.make_async_copy(slots_v, out, sem).wait()
 
 
 def near_sum(blocks, got):
+    shape = (NY * NX, SLOTS, HALF, SIDE)
     return pl.pallas_call(
         near_sum_kernel,
         in_specs=[SMEM, VMEM],
-        out_specs=VMEM,
-        out_shape=jax.ShapeDtypeStruct((NY * NX, SLOTS, HALF, SIDE), bf16),
-        scratch_shapes=[pltpu.VMEM((BLOCKS + 1, HALF, SIDE), bf16)],
+        out_specs=HBM,
+        out_shape=jax.ShapeDtypeStruct(shape, bf16),
+        scratch_shapes=[
+            pltpu.VMEM((BLOCKS + 1, HALF, SIDE), bf16),
+            pltpu.VMEM(shape, bf16),
+            pltpu.SemaphoreType.DMA,
+        ],
         compiler_params=params(16),
         cost_estimate=cost(got.size, 3 * MIB),
     )(blocks, got)
@@ -119,9 +128,14 @@
             for y in range(odd_y, NY, PAIR):
                 for x in range(odd_x, NX, PAIR):
                     total += got[y * NX + x].astype(f32)
-            row = pl.ds(pl.multiple_of(lax.rem(odd_y + core, PAIR) * HALF, HALF), HALF)
-            col = pl.ds(pl.multiple_of(lax.rem(odd_x + core, PAIR) * SIDE, SIDE), SIDE)
-            total_v[:, row, col] = total.astype(bf16)
+            total = total.astype(bf16)
+            for c in range(NC):
+                top, left = (odd_y + c) % PAIR, (odd_x + c) % PAIR
+
+                @pl.when(core == c)
+                def _():
+                    total_v[:, top * HALF:(top + 1) * HALF, left * SIDE:(left + 1) * SIDE] = total
+
     for z in range(NZ):
         pltpu.make_async_copy(total_v, out.at[z], sem).start()
     pltpu.make_async_copy(out, out, sem).wait()
@@ -250,7 +264,7 @@
     part = near_sum(jnp.where(slot_blocks < BLOCKS, place_of, BLOCKS), part)
     part, r1 = after(part, r1)
     r2 = jump(r1, 1)
-    r3 = jump(r2, 1)
+    r3 = jump(r1, 2)
     part = last_sum(place, exchange(part, ("y", "x")))
     part, r2, r3 = after(part, r2, r3)
     r4 = jump(r3, 1)

time: 87.6 us -> 87.6 us (level)
  starting transfers between devices: 58 us -> 56 us
  waiting for transfers between devices: 16.1 us -> 18.1 us
    all_to_all x3, waiting for transfers between devices: 0.6 us -> 7.05 us  [exchange(): lax.all_to_all(value, axes, 0, 0, axis_index_groups=groups, tiled=True)]
    ppermute x4, waiting for transfers between devices: 13.7 us -> 9.25 us  [jump(): return lax.ppermute(value, ('z', 'core'), pairs)]
    ppermute x4, starting transfers between devices: 26.1 us -> 23 us  [jump(): return lax.ppermute(value, ('z', 'core'), pairs)]
    all_to_all x3, starting transfers between devices: 21.1 us -> 22.3 us  [exchange(): lax.all_to_all(value, axes, 0, 0, axis_index_groups=groups, tiled=True)]
  transfers between devices with their start and end apart: 10 -> 10, of which waited for: 7 -> 5; matrix products, arithmetic and copies ran while one was open for 0% -> 0% of each run, Pallas kernels for 4% -> 4%
where the time goes in v5:
time: 87.6 us; the launch traced here: 87 us
  starting transfers between devices  56 us (64%)
  waiting for transfers between devices  18.1 us (21%)
  Pallas kernels  11.8 us (13%)
    ppermute x4, starting transfers between devices, jump(): return lax.ppermute(value, ('z', 'core'), pairs)  23 us
    all_to_all x3, starting transfers between devices, exchange(): lax.all_to_all(value, axes, 0, 0, axis_index_groups=groups, tiled=True)  22.3 us
    ppermute x3, starting transfers between devices, swap(): return lax.ppermute(value, 'core', [(0, 1), (1, 0)])  10.8 us
    ppermute x4, waiting for transfers between devices, jump(): return lax.ppermute(value, ('z', 'core'), pairs)  9.25 us
    all_to_all x3, waiting for transfers between devices, exchange(): lax.all_to_all(value, axes, 0, 0, axis_index_groups=groups, tiled=True)  7.05 us
    pallas_call x1, Pallas kernels, cut_partials(): pl.pallas_call(partial_kernel, in_specs=[HBM, HBM], out_specs=HBM, out_sh...  4.55 us
    pallas_call x1, Pallas kernels, final(): pl.pallas_call(final_kernel, in_specs=[SMEM] + [VMEM] * 5, out_specs=(VME...  3.47 us
    ppermute x3, waiting for transfers between devices, swap(): return lax.ppermute(value, 'core', [(0, 1), (1, 0)])  1.78 us
  transfers between devices with their start and end apart: 10, of which 5 were waited for; matrix products, arithmetic and copies ran while one was open for 0% of the time, Pallas kernels for 4%

profile of v5, /device:TPU:1, one launch (start us, length us, event | category | flops | bytes accessed | tf_op | source)
XLA Modules:
  0.0 87.0 jit_solution(7558755300993439864)
XLA Ops:
  0.6 4.6 %shard_map.94 = bf16[4,48,16,256]{3,2,1,0:T(8,128)(2,1)} custom-call(bf16[24,32,1024]{2,1,0:T(8,128)(2,1)} %act.1, bf16[1024,1024]{1,0:T(8,128)(2,1)} %cot.1), custom_call_target="tpu_custom_call" | custom-call | flops 1610612736 | bytes 6291456 | tf_op jit(solution)/shard_map/pallas_call | solution.py:73
  5.2 0.0 copy-start.2
  5.2 0.0 copy-start.3
  5.2 0.0 copy-start.4
  5.2 9.9 %all-to-all-start = ((bf16[4,48,16,256]{3,2,1,0:T(8,128)(2,1)}), bf16[4,48,16,256]{3,2,1,0:T(8,128)(2,1)S(1)}, u32[]{:S(2)}, u32[]{:S(2)}) async-start(bf16[4,48,16,256]{3,2,1,0:T(8,128)(2,1)} %shard_map.94), calls=%async_computation | async-start | bytes 3145728 | tf_op jit(solution)/shard_map/all_to_all | solution.py:240
  15.1 0.0 copy-done.2
  15.1 0.0 copy-done.3
  15.1 2.6 %collective-permute-start = (bf16[2,2,32,512]{3,2,1,0:T(8,128)(2,1)S(1)}, bf16[2,2,32,512]{3,2,1,0:T(8,128)(2,1)S(1)}, u32[]{:S(2)}, u32[]{:S(2)}) collective-permute-start(bf16[2,2,32,512]{3,2,1,0:T(8,128)(2,1)S(1)} %get-tuple-element.18), channel_id=1, source_target_pairs={{0,1},{1,0},{2,3},{3,2},{4,5},{5,4},{6,7},{7,6},{8,9},{9,8},{10,11... | collective-permute-start | bytes 393224 | tf_op jit(solution)/shard_map/ppermute | solution.py:228
  17.8 1.0 %collective-permute-done = bf16[2,2,32,512]{3,2,1,0:T(8,128)(2,1)S(1)} collective-permute-done((bf16[2,2,32,512]{3,2,1,0:T(8,128)(2,1)S(1)}, bf16[2,2,32,512]{3,2,1,0:T(8,128)(2,1)S(1)}, u32[]{:S(2)}, u32[]{:S(2)}) %collective-permute-start) | collective-permute-done | bytes 131104 | tf_op jit(solution)/shard_map/ppermute | solution.py:228
  18.8 10.3 %collective-permute-start.1 = (bf16[2,2,2,32,512]{4,3,2,1,0:T(8,128)(2,1)S(1)}, bf16[2,2,2,32,512]{4,3,2,1,0:T(8,128)(2,1)S(1)}, u32[]{:S(2)}, u32[]{:S(2)}) collective-permute-start(bf16[2,2,2,32,512]{4,3,2,1,0:T(8,128)(2,1)S(1)} %pad_maximum_fusion.1.here), channel_id=1, source_target_pairs={{0,2},{1,15},{2,4},{3,1},{4,6},{5,3},{6,8},{7,5},{8,10},{9,7},{10,... | collective-permute-start | bytes 786440 | tf_op jit(solution)/shard_map/ppermute | solution.py:236
  29.1 0.0 copy-done.4
  29.1 0.0 all-to-all-done.got
  29.1 1.7 %shard_map.95 = bf16[32,2,16,256]{3,2,1,0:T(8,128)(2,1)} custom-call(s32[64]{0:T(128)S(1)} %compare_select_fusion.blocks, bf16[4,48,16,256]{3,2,1,0:T(8,128)(2,1)S(1)} %all-to-all-done.got), custom_call_target="tpu_custom_call" | custom-call | flops 786432 | bytes 3145728 | tf_op jit(solution)/shard_map/pallas_call | solution.py:108
  30.8 1.6 %collective-permute-done.1 = bf16[2,2,2,32,512]{4,3,2,1,0:T(8,128)(2,1)S(1)} collective-permute-done((bf16[2,2,2,32,512]{4,3,2,1,0:T(8,128)(2,1)S(1)}, bf16[2,2,2,32,512]{4,3,2,1,0:T(8,128)(2,1)S(1)}, u32[]{:S(2)}, u32[]{:S(2)}) %collective-permute-start.1) | collective-permute-done | bytes 262176 | tf_op jit(solution)/shard_map/ppermute | solution.py:236
  32.4 5.6 %all-to-all-start.1 = ((bf16[32,2,16,256]{3,2,1,0:T(8,128)(2,1)}), bf16[32,2,16,256]{3,2,1,0:T(8,128)(2,1)S(1)}, u32[]{:S(2)}, u32[]{:S(2)}) async-start(bf16[32,2,16,256]{3,2,1,0:T(8,128)(2,1)} %shard_map.95), calls=%async_computation.1 | async-start | bytes 1048576 | tf_op jit(solution)/shard_map/all_to_all | solution.py:240
  38.0 5.9 %collective-permute-start.2 = (bf16[2,2,2,32,512]{4,3,2,1,0:T(8,128)(2,1)S(1)}, bf16[2,2,2,32,512]{4,3,2,1,0:T(8,128)(2,1)S(1)}, u32[]{:S(2)}, u32[]{:S(2)}) collective-permute-start(bf16[2,2,2,32,512]{4,3,2,1,0:T(8,128)(2,1)S(1)} %collective-permute-done.1), channel_id=1, source_target_pairs={{0,2},{1,15},{2,4},{3,1},{4,6},{5,3},{6,8},{7,5},{8,10},{9,7},{10,... | collective-permute-start | bytes 786440 | tf_op jit(solution)/shard_map/ppermute | solution.py:236
  43.9 2.2 %collective-permute-start.3 = (bf16[2,2,2,32,512]{4,3,2,1,0:T(8,128)(2,1)S(1)}, bf16[2,2,2,32,512]{4,3,2,1,0:T(8,128)(2,1)S(1)}, u32[]{:S(2)}, u32[]{:S(2)}) collective-permute-start(bf16[2,2,2,32,512]{4,3,2,1,0:T(8,128)(2,1)S(1)} %collective-permute-done.1), channel_id=1, source_target_pairs={{0,4},{1,13},{2,6},{3,15},{4,8},{5,1},{6,10},{7,3},{8,12},{9,5},{1... | collective-permute-start | bytes 786440 | tf_op jit(solution)/shard_map/ppermute | solution.py:236
  46.1 0.1 pad_add_fusion.place
  46.2 7.0 %all-to-all-done.1.got = bf16[32,2,16,256]{3,2,1,0:T(8,128)(2,1)S(1)} async-done(((bf16[32,2,16,256]{3,2,1,0:T(8,128)(2,1)}), bf16[32,2,16,256]{3,2,1,0:T(8,128)(2,1)S(1)}, u32[]{:S(2)}, u32[]{:S(2)}) %all-to-all-start.1) | async-done | bytes 524320 | tf_op jit(solution)/shard_map/all_to_all | solution.py:240
  53.2 1.4 %shard_map.96 = bf16[8,2,32,512]{3,2,1,0:T(8,128)(2,1)} custom-call(s32[2]{0:T(128)S(1)} %pad_add_fusion.place, bf16[32,2,16,256]{3,2,1,0:T(8,128)(2,1)S(1)} %all-to-all-done.1.got), custom_call_target="tpu_custom_call" | custom-call | flops 262144 | bytes 1048576 | tf_op jit(solution)/shard_map/pallas_call | solution.py:146
  54.6 0.0 collective-permute-done.2
  54.7 0.0 collective-permute-done.3
  54.7 6.8 %all-to-all-start.2 = ((bf16[8,2,32,512]{3,2,1,0:T(8,128)(2,1)}), bf16[8,2,32,512]{3,2,1,0:T(8,128)(2,1)S(1)}, u32[]{:S(2)}, u32[]{:S(2)}) async-start(bf16[8,2,32,512]{3,2,1,0:T(8,128)(2,1)} %shard_map.96), calls=%async_computation.2 | async-start | bytes 1048576 | tf_op jit(solution)/shard_map/all_to_all | solution.py:240
  61.4 4.6 %collective-permute-start.4 = (bf16[2,2,2,32,512]{4,3,2,1,0:T(8,128)(2,1)S(1)}, bf16[2,2,2,32,512]{4,3,2,1,0:T(8,128)(2,1)S(1)}, u32[]{:S(2)}, u32[]{:S(2)}) collective-permute-start(bf16[2,2,2,32,512]{4,3,2,1,0:T(8,128)(2,1)S(1)} %collective-permute-done.3), channel_id=1, source_target_pairs={{0,2},{1,15},{2,4},{3,1},{4,6},{5,3},{6,8},{7,5},{8,10},{9,7},{10,... | collective-permute-start | bytes 786440 | tf_op jit(solution)/shard_map/ppermute | solution.py:236
  66.0 0.1 pad_maximum_fusion.own
  66.1 0.0 copy-start
  66.1 0.0 copy-start.1
  66.1 4.0 %collective-permute-start.6 = (bf16[3,2,2,2,32,512]{5,4,3,2,1,0:T(8,128)(2,1)S(1)}, bf16[3,2,2,2,32,512]{5,4,3,2,1,0:T(8,128)(2,1)S(1)}, u32[]{:S(2)}, u32[]{:S(2)}) collective-permute-start(bf16[3,2,2,2,32,512]{5,4,3,2,1,0:T(8,128)(2,1)S(1)} %pad_maximum_fusion.own), channel_id=1, source_target_pairs={{0,1},{1,0},{2,3},{3,2},{4,5},{5,4},{6,7},{7,6},{8,9},{9,8},{10,11... | collective-permute-start | bytes 2359304 | tf_op jit(solution)/shard_map/ppermute | solution.py:228
  70.1 7.7 %collective-permute-done.4.far = bf16[2,2,2,32,512]{4,3,2,1,0:T(8,128)(2,1)S(1)} collective-permute-done((bf16[2,2,2,32,512]{4,3,2,1,0:T(8,128)(2,1)S(1)}, bf16[2,2,2,32,512]{4,3,2,1,0:T(8,128)(2,1)S(1)}, u32[]{:S(2)}, u32[]{:S(2)}) %collective-permute-start.4) | collective-permute-done | bytes 262176 | tf_op jit(solution)/shard_map/ppermute | solution.py:236
  77.8 0.0 all-to-all-done.2.g_own
  77.8 4.2 %collective-permute-start.5 = (bf16[8,2,32,512]{3,2,1,0:T(8,128)(2,1)S(1)}, bf16[8,2,32,512]{3,2,1,0:T(8,128)(2,1)S(1)}, u32[]{:S(2)}, u32[]{:S(2)}) collective-permute-start(bf16[8,2,32,512]{3,2,1,0:T(8,128)(2,1)S(1)} %all-to-all-done.2.g_own), channel_id=1, source_target_pairs={{0,1},{1,0},{2,3},{3,2},{4,5},{5,4},{6,7},{7,6},{8,9},{9,8},{10,11... | collective-permute-start | bytes 1572872 | tf_op jit(solution)/shard_map/ppermute | solution.py:228
  82.0 0.0 collective-permute-done.6.other
  82.0 0.7 shard_map.97.w
  82.7 0.8 collective-permute-done.5.g_other
  83.5 0.0 copy-done
  83.5 0.0 copy-done.1
  83.5 3.5 %shard_map.98 = (f32[2,32,512]{2,1,0:T(8,128)}, f32[2,32,512]{2,1,0:T(8,128)}, bf16[2,512,512]{2,1,0:T(8,128)(2,1)}) custom-call(s32[2]{0:T(128)S(1)} %pad_add_fusion.place, bf16[8,2,32,512]{3,2,1,0:T(8,128)(2,1)S(1)} %all-to-all-done.2.g_own, bf16[8,2,32,512]{3,2,1,0:T(8,128)(2,1)S(1)} %collective-permute-done.5.g_other, ...), custom_call_target="tpu_custom_call" | custom-call | flops 1200000000 | bytes 8388608 | tf_op jit(solution)/shard_map/pallas_call | solution.py:212
  (3 shorter events, 0.1 us)
Async XLA Ops:
  5.2 9.9 %copy-start.2 = (bf16[2,32,512]{2,1,0:T(8,128)(2,1)S(1)}, bf16[2,32,512]{2,1,0:T(8,128)(2,1)}, u32[]{:S(2)}) copy-start(bf16[2,32,512]{2,1,0:T(8,128)(2,1)} %param.13) | copy-start | bytes 196612
  5.2 9.9 %copy-start.3 = (bf16[2,32,512]{2,1,0:T(8,128)(2,1)S(1)}, bf16[2,32,512]{2,1,0:T(8,128)(2,1)}, u32[]{:S(2)}) copy-start(bf16[2,32,512]{2,1,0:T(8,128)(2,1)} %param.12) | copy-start | bytes 196612
  5.2 23.9 %copy-start.4 = (s32[64]{0:T(128)S(1)}, s32[64]{0:T(128)}, u32[]{:S(2)}) copy-start(s32[64]{0:T(128)} %param.9) | copy-start | bytes 772
  5.2 23.9 %all-to-all-start = ((bf16[4,48,16,256]{3,2,1,0:T(8,128)(2,1)}), bf16[4,48,16,256]{3,2,1,0:T(8,128)(2,1)S(1)}, u32[]{:S(2)}, u32[]{:S(2)}) async-start(bf16[4,48,16,256]{3,2,1,0:T(8,128)(2,1)} %shard_map.94), calls=%async_computation | async-start | bytes 3145728 | tf_op jit(solution)/shard_map/all_to_all | solution.py:240
  15.1 3.6 %collective-permute-start = (bf16[2,2,32,512]{3,2,1,0:T(8,128)(2,1)S(1)}, bf16[2,2,32,512]{3,2,1,0:T(8,128)(2,1)S(1)}, u32[]{:S(2)}, u32[]{:S(2)}) collective-permute-start(bf16[2,2,32,512]{3,2,1,0:T(8,128)(2,1)S(1)} %get-tuple-element.18), channel_id=1, source_target_pairs={{0,1},{1,0},{2,3},{3,2},{4,5},{5,4},{6,7},{7,6},{8,9},{9,8},{10,11... | collective-permute-start | bytes 393224 | tf_op jit(solution)/shard_map/ppermute | solution.py:228
  18.8 13.6 %collective-permute-start.1 = (bf16[2,2,2,32,512]{4,3,2,1,0:T(8,128)(2,1)S(1)}, bf16[2,2,2,32,512]{4,3,2,1,0:T(8,128)(2,1)S(1)}, u32[]{:S(2)}, u32[]{:S(2)}) collective-permute-start(bf16[2,2,2,32,512]{4,3,2,1,0:T(8,128)(2,1)S(1)} %pad_maximum_fusion.1.here), channel_id=1, source_target_pairs={{0,2},{1,15},{2,4},{3,1},{4,6},{5,3},{6,8},{7,5},{8,10},{9,7},{10,... | collective-permute-start | bytes 786440 | tf_op jit(solution)/shard_map/ppermute | solution.py:236
  32.4 20.8 %all-to-all-start.1 = ((bf16[32,2,16,256]{3,2,1,0:T(8,128)(2,1)}), bf16[32,2,16,256]{3,2,1,0:T(8,128)(2,1)S(1)}, u32[]{:S(2)}, u32[]{:S(2)}) async-start(bf16[32,2,16,256]{3,2,1,0:T(8,128)(2,1)} %shard_map.95), calls=%async_computation.1 | async-start | bytes 1048576 | tf_op jit(solution)/shard_map/all_to_all | solution.py:240
  38.0 16.7 %collective-permute-start.2 = (bf16[2,2,2,32,512]{4,3,2,1,0:T(8,128)(2,1)S(1)}, bf16[2,2,2,32,512]{4,3,2,1,0:T(8,128)(2,1)S(1)}, u32[]{:S(2)}, u32[]{:S(2)}) collective-permute-start(bf16[2,2,2,32,512]{4,3,2,1,0:T(8,128)(2,1)S(1)} %collective-permute-done.1), channel_id=1, source_target_pairs={{0,2},{1,15},{2,4},{3,1},{4,6},{5,3},{6,8},{7,5},{8,10},{9,7},{10,... | collective-permute-start | bytes 786440 | tf_op jit(solution)/shard_map/ppermute | solution.py:236
  43.9 10.7 %collective-permute-start.3 = (bf16[2,2,2,32,512]{4,3,2,1,0:T(8,128)(2,1)S(1)}, bf16[2,2,2,32,512]{4,3,2,1,0:T(8,128)(2,1)S(1)}, u32[]{:S(2)}, u32[]{:S(2)}) collective-permute-start(bf16[2,2,2,32,512]{4,3,2,1,0:T(8,128)(2,1)S(1)} %collective-permute-done.1), channel_id=1, source_target_pairs={{0,4},{1,13},{2,6},{3,15},{4,8},{5,1},{6,10},{7,3},{8,12},{9,5},{1... | collective-permute-start | bytes 786440 | tf_op jit(solution)/shard_map/ppermute | solution.py:236
  54.7 23.1 %all-to-all-start.2 = ((bf16[8,2,32,512]{3,2,1,0:T(8,128)(2,1)}), bf16[8,2,32,512]{3,2,1,0:T(8,128)(2,1)S(1)}, u32[]{:S(2)}, u32[]{:S(2)}) async-start(bf16[8,2,32,512]{3,2,1,0:T(8,128)(2,1)} %shard_map.96), calls=%async_computation.2 | async-start | bytes 1048576 | tf_op jit(solution)/shard_map/all_to_all | solution.py:240
  61.4 16.4 %collective-permute-start.4 = (bf16[2,2,2,32,512]{4,3,2,1,0:T(8,128)(2,1)S(1)}, bf16[2,2,2,32,512]{4,3,2,1,0:T(8,128)(2,1)S(1)}, u32[]{:S(2)}, u32[]{:S(2)}) collective-permute-start(bf16[2,2,2,32,512]{4,3,2,1,0:T(8,128)(2,1)S(1)} %collective-permute-done.3), channel_id=1, source_target_pairs={{0,2},{1,15},{2,4},{3,1},{4,6},{5,3},{6,8},{7,5},{8,10},{9,7},{10,... | collective-permute-start | bytes 786440 | tf_op jit(solution)/shard_map/ppermute | solution.py:236
  66.1 17.4 %copy-start = (f32[2,32,512]{2,1,0:T(8,128)S(1)}, f32[2,32,512]{2,1,0:T(8,128)}, u32[]{:S(2)}) copy-start(f32[2,32,512]{2,1,0:T(8,128)} %left_stat.1) | copy-start | bytes 393220
  66.1 17.4 %copy-start.1 = (f32[2,32,512]{2,1,0:T(8,128)S(1)}, f32[2,32,512]{2,1,0:T(8,128)}, u32[]{:S(2)}) copy-start(f32[2,32,512]{2,1,0:T(8,128)} %right_stat.1) | copy-start | bytes 393220
  66.1 15.9 %collective-permute-start.6 = (bf16[3,2,2,2,32,512]{5,4,3,2,1,0:T(8,128)(2,1)S(1)}, bf16[3,2,2,2,32,512]{5,4,3,2,1,0:T(8,128)(2,1)S(1)}, u32[]{:S(2)}, u32[]{:S(2)}) collective-permute-start(bf16[3,2,2,2,32,512]{5,4,3,2,1,0:T(8,128)(2,1)S(1)} %pad_maximum_fusion.own), channel_id=1, source_target_pairs={{0,1},{1,0},{2,3},{3,2},{4,5},{5,4},{6,7},{7,6},{8,9},{9,8},{10,11... | collective-permute-start | bytes 2359304 | tf_op jit(solution)/shard_map/ppermute | solution.py:228
  77.8 5.7 %collective-permute-start.5 = (bf16[8,2,32,512]{3,2,1,0:T(8,128)(2,1)S(1)}, bf16[8,2,32,512]{3,2,1,0:T(8,128)(2,1)S(1)}, u32[]{:S(2)}, u32[]{:S(2)}) collective-permute-start(bf16[8,2,32,512]{3,2,1,0:T(8,128)(2,1)S(1)} %all-to-all-done.2.g_own), channel_id=1, source_target_pairs={{0,1},{1,0},{2,3},{3,2},{4,5},{5,4},{6,7},{7,6},{8,9},{9,8},{10,11... | collective-permute-start | bytes 1572872 | tf_op jit(solution)/shard_map/ppermute | solution.py:228
